TPU v7x, 128 devices: a whole 4x4x4 slice. The times are simulated.
128 devices in a mesh: dp: 64 (over z_hi, x, y, core), tensor: 2 (over z_lo).
Axes of the slice: x: 4, y: 4, z: 4 (z_hi: 2, z_lo: 2; z = z_hi * 2 + z_lo), core: 2. Of those that a mesh axis runs over, the one named last changes fastest.
Arguments:
- layer_input: bfloat16 [32768, 768], P('dp'), may hold values from -6 to 6
- seg_ids: int32 [32768], P('dp'), may hold values from 0 to 127, never falling along the last dimension, each value on 1 to 2048 neighbouring positions
- ln1_gain: float32 [768], replicated, may hold values from 0.5 to 1.5
- ln1_bias: float32 [768], replicated, may hold values from -2.5 to 2.5
- ln2_gain: float32 [768], replicated, may hold values from 0.5 to 1.5
- ln2_bias: float32 [768], replicated, may hold values from -2.5 to 2.5
- w_qkv: bfloat16 [768, 12, 192], P(None, 'tensor'), may hold values from -0.21875 to 0.21875
- b_qkv: float32 [12, 192], P('tensor'), may hold values from -2.5 to 2.5
- w_out: bfloat16 [12, 64, 768], P('tensor'), may hold values from -0.625 to 0.625
- b_out: float32 [768], replicated, may hold values from -2.5 to 2.5
- w_fc: bfloat16 [768, 3072], P(None, 'tensor'), may hold values from -0.21875 to 0.21875
- b_fc: float32 [3072], P('tensor'), may hold values from -2.5 to 2.5
- w_proj: bfloat16 [3072, 768], P('tensor'), may hold values from -0.109375 to 0.109375
- b_proj: float32 [768], replicated, may hold values from -2.5 to 2.5
- cotangent: float32 [32768, 768], P('dp'), may hold values from -6 to 6
Outputs:
- layer_output: bfloat16 [32768, 768], P('dp')
- grad_input: float32 [32768, 768], P('dp')
- grad_ln1_gain: float32 [768], replicated
- grad_ln1_bias: float32 [768], replicated
- grad_ln2_gain: float32 [768], replicated
- grad_ln2_bias: float32 [768], replicated
- grad_w_qkv: float32 [768, 12, 192], P(None, 'tensor')
- grad_b_qkv: float32 [12, 192], P('tensor')
- grad_w_out: float32 [12, 64, 768], P('tensor')
- grad_b_out: float32 [768], replicated
- grad_w_fc: float32 [768, 3072], P(None, 'tensor')
- grad_b_fc: float32 [3072], P('tensor')
- grad_w_proj: float32 [3072, 768], P('tensor')
- grad_b_proj: float32 [768], replicated
Inputs may be any that keep to these rules, and one draw needn't show every extreme that they name: `seg_ids`: document numbers never fall from one token to the next.
All inputs are finite; a program needn't handle non-finite values.
Results may differ from a plain program's by a relative error of at most 0.0098.
Values may be sent and summed in bfloat16 or wider, within the bound.
No kernel may reach another device: no remote copies, remote signals or barrier semaphores. Data moves between devices by JAX's collectives and lax.ppermute only.
A program may use at most 128 MiB of HBM per device.

v0:
```python
import jax
import jax.numpy as jnp
from jax import lax
from jax.sharding import PartitionSpec as P

HD = 64
ROT = 16
SEQ = 512


epsilon = 1e-05
masked_score = -1000000000.0


def norm_rows(row_values, gain_vec, shift_vec):
    row_mean = jnp.mean(row_values, axis=-1, keepdims=True)
    centred = row_values - row_mean
    variance = jnp.mean(centred * centred, axis=-1, keepdims=True)
    return centred * lax.rsqrt(variance + epsilon) * gain_vec + shift_vec


def rotate(row_values, cosine_table, sine_table):
    half_rot = ROT // 2
    leading = row_values[..., :half_rot]
    trailing = row_values[..., half_rot:ROT]
    cosine_col = cosine_table[:, None, :]
    sine_col = sine_table[:, None, :]
    return jnp.concatenate(
        [
            leading * cosine_col - trailing * sine_col,
            trailing * cosine_col + leading * sine_col,
            row_values[..., ROT:],
        ],
        axis=-1,
    )


def tables(segments):
    indices = jnp.arange(SEQ, dtype=jnp.int32)
    starts = jnp.concatenate([jnp.ones((1,), dtype=bool), segments[1:] != segments[:-1]])
    opening = lax.cummax(jnp.where(starts, indices, 0), axis=0)
    offset = (indices - opening).astype(jnp.float32)
    frequency = 10000.0 ** (jnp.arange(ROT // 2).astype(jnp.float32) * (-2.0 / ROT))
    angles = offset[:, None] * frequency[None, :]
    allowed = (segments[:, None] == segments[None, :]) & (indices[:, None] >= indices[None, :])
    return (jnp.cos(angles), jnp.sin(angles), allowed)


def gelu_exact(row_values):
    return jax.nn.gelu(row_values, approximate=False)


def contract_rows(left_mat, right_mat):
    return lax.dot_general(
        left_mat, right_mat, (((0,), (0,)), ((), ())), preferred_element_type=jnp.float32
    )


def contract_cols(left_mat, right_mat):
    return lax.dot_general(
        left_mat, right_mat, (((1,), (1,)), ((), ())), preferred_element_type=jnp.float32
    )


def body(
    layer_input,
    seg_ids,
    ln1_gain,
    ln1_bias,
    ln2_gain,
    ln2_bias,
    w_qkv,
    b_qkv,
    w_out,
    b_out,
    w_fc,
    b_fc,
    w_proj,
    b_proj,
    cotangent,
):
    tok_rows = layer_input.shape[0]
    model_width = layer_input.shape[1]
    head_count = w_qkv.shape[1]
    seq_count = tok_rows // SEQ
    score_scale = HD ** (-0.5)
    x_float = layer_input.astype(jnp.float32)
    normed_attn, pull_attn = jax.vjp(norm_rows, x_float, ln1_gain, ln1_bias)
    normed_mlp, pull_mlp = jax.vjp(norm_rows, x_float, ln2_gain, ln2_bias)
    attn_in = normed_attn.astype(jnp.bfloat16)
    mlp_in = normed_mlp.astype(jnp.bfloat16)
    flat_qkv = w_qkv.reshape(model_width, head_count * 3 * HD)
    mixed_qkv = (
        jnp.dot(attn_in, flat_qkv, preferred_element_type=jnp.float32).reshape(
            tok_rows, head_count, 3 * HD
        )
        + b_qkv
    )
    hidden = jnp.dot(mlp_in, w_fc, preferred_element_type=jnp.float32) + b_fc
    activated, pull_gelu = jax.vjp(gelu_exact, hidden)
    act_low = activated.astype(jnp.bfloat16)
    seg_blocks = seg_ids.reshape(seq_count, SEQ)

    def attend_forward(packed):
        mixed_seq, segments = packed
        cosine_table, sine_table, allowed = tables(segments)
        queries = rotate(mixed_seq[..., :HD], cosine_table, sine_table).astype(jnp.bfloat16)
        keys_rot = rotate(mixed_seq[..., HD : 2 * HD], cosine_table, sine_table).astype(
            jnp.bfloat16
        )
        values = mixed_seq[..., 2 * HD :].astype(jnp.bfloat16)
        scores = (
            jnp.einsum("qhd,khd->hqk", queries, keys_rot, preferred_element_type=jnp.float32)
            * score_scale
        )
        scores = jnp.where(allowed[None], scores, masked_score)
        row_top = jnp.max(scores, axis=-1, keepdims=True)
        powers = jnp.exp(scores - row_top)
        totals = jnp.sum(powers, axis=-1, keepdims=True)
        weights = (powers / totals).astype(jnp.bfloat16)
        context = jnp.einsum("hqk,khd->qhd", weights, values, preferred_element_type=jnp.float32)
        return (context.astype(jnp.bfloat16), row_top + jnp.log(totals), queries, keys_rot, values)

    context, log_totals, queries_all, keys_all, values_all = lax.map(
        attend_forward, (mixed_qkv.reshape(seq_count, SEQ, head_count, 3 * HD), seg_blocks)
    )
    context_flat = context.reshape(tok_rows, head_count * HD)
    flat_out = w_out.reshape(head_count * HD, model_width)
    partial_value = jnp.dot(context_flat, flat_out, preferred_element_type=jnp.float32) + jnp.dot(
        act_low, w_proj, preferred_element_type=jnp.float32
    )
    output = (
        x_float
        + lax.psum(partial_value.astype(jnp.bfloat16), "tensor").astype(jnp.float32)
        + b_out
        + b_proj
    ).astype(jnp.bfloat16)
    grad_low = cotangent.astype(jnp.bfloat16)
    grad_shift = jnp.sum(cotangent, axis=0)
    grad_w_proj = contract_rows(act_low, grad_low)
    grad_act = contract_cols(grad_low, w_proj)
    grad_hidden = pull_gelu(grad_act)[0].astype(jnp.bfloat16)
    grad_b_fc = jnp.sum(grad_hidden, axis=0, dtype=jnp.float32)
    grad_w_fc = contract_rows(mlp_in, grad_hidden)
    grad_mlp_in = contract_cols(grad_hidden, w_fc)
    grad_w_out = contract_rows(context_flat, grad_low).reshape(w_out.shape)
    grad_context = (
        contract_cols(grad_low, flat_out)
        .astype(jnp.bfloat16)
        .reshape(seq_count, SEQ, head_count, HD)
    )

    def attend_backward(packed):
        queries, keys_rot, values, log_seq, grad_seq, segments = packed
        cosine_table, sine_table, allowed = tables(segments)
        scores = (
            jnp.einsum("qhd,khd->hqk", queries, keys_rot, preferred_element_type=jnp.float32)
            * score_scale
        )
        scores = jnp.where(allowed[None], scores, masked_score)
        probabilities = jnp.exp(scores - log_seq)
        grad_values = jnp.einsum(
            "hqk,qhd->khd",
            probabilities.astype(jnp.bfloat16),
            grad_seq,
            preferred_element_type=jnp.float32,
        )
        grad_probs = jnp.einsum(
            "qhd,khd->hqk", grad_seq, values, preferred_element_type=jnp.float32
        )
        grad_scores = (
            probabilities
            * (grad_probs - jnp.sum(probabilities * grad_probs, axis=-1, keepdims=True))
        ).astype(jnp.bfloat16)
        grad_queries = (
            jnp.einsum("hqk,khd->qhd", grad_scores, keys_rot, preferred_element_type=jnp.float32)
            * score_scale
        )
        grad_keys = (
            jnp.einsum("hqk,qhd->khd", grad_scores, queries, preferred_element_type=jnp.float32)
            * score_scale
        )
        return jnp.concatenate(
            [
                rotate(grad_queries, cosine_table, -sine_table),
                rotate(grad_keys, cosine_table, -sine_table),
                grad_values,
            ],
            axis=-1,
        )

    grad_mixed = lax.map(
        attend_backward, (queries_all, keys_all, values_all, log_totals, grad_context, seg_blocks)
    )
    grad_mixed = grad_mixed.reshape(tok_rows, head_count * 3 * HD).astype(jnp.bfloat16)
    grad_b_qkv = jnp.sum(grad_mixed, axis=0, dtype=jnp.float32).reshape(head_count, 3 * HD)
    grad_w_qkv = contract_rows(attn_in, grad_mixed).reshape(w_qkv.shape)
    grad_attn_in = contract_cols(grad_mixed, flat_qkv)
    grad_x_attn, grad_gain_attn, grad_bias_attn = pull_attn(grad_attn_in)
    grad_x_mlp, grad_gain_mlp, grad_bias_mlp = pull_mlp(grad_mlp_in)
    summed_x, gain_attn, bias_attn, gain_mlp, bias_mlp = (
        lax.psum((grad_x_attn + grad_x_mlp).astype(jnp.bfloat16), "tensor").astype(jnp.float32),
        lax.psum(grad_gain_attn.astype(jnp.bfloat16), "tensor").astype(jnp.float32),
        lax.psum(grad_bias_attn.astype(jnp.bfloat16), "tensor").astype(jnp.float32),
        lax.psum(grad_gain_mlp.astype(jnp.bfloat16), "tensor").astype(jnp.float32),
        lax.psum(grad_bias_mlp.astype(jnp.bfloat16), "tensor").astype(jnp.float32),
    )
    grad_x = cotangent + summed_x
    shares = (
        lax.psum_scatter(grad_w_qkv, "dp", scatter_dimension=0, tiled=True),
        lax.psum_scatter(grad_b_qkv, "dp", scatter_dimension=1, tiled=True),
        lax.psum_scatter(grad_w_out, "dp", scatter_dimension=2, tiled=True),
        lax.psum_scatter(grad_w_fc, "dp", scatter_dimension=0, tiled=True),
        lax.psum_scatter(grad_b_fc, "dp", scatter_dimension=0, tiled=True),
        lax.psum_scatter(grad_w_proj, "dp", scatter_dimension=1, tiled=True),
        lax.psum_scatter(grad_shift, "dp", scatter_dimension=0, tiled=True),
        lax.psum_scatter(gain_attn, "dp", scatter_dimension=0, tiled=True),
        lax.psum_scatter(bias_attn, "dp", scatter_dimension=0, tiled=True),
        lax.psum_scatter(gain_mlp, "dp", scatter_dimension=0, tiled=True),
        lax.psum_scatter(bias_mlp, "dp", scatter_dimension=0, tiled=True),
    )
    whole_grads = (
        lax.all_gather(shares[0].astype(jnp.bfloat16), "dp", axis=0, tiled=True).astype(
            jnp.float32
        ),
        lax.all_gather(shares[1].astype(jnp.bfloat16), "dp", axis=1, tiled=True).astype(
            jnp.float32
        ),
        lax.all_gather(shares[2].astype(jnp.bfloat16), "dp", axis=2, tiled=True).astype(
            jnp.float32
        ),
        lax.all_gather(shares[3].astype(jnp.bfloat16), "dp", axis=0, tiled=True).astype(
            jnp.float32
        ),
        lax.all_gather(shares[4].astype(jnp.bfloat16), "dp", axis=0, tiled=True).astype(
            jnp.float32
        ),
        lax.all_gather(shares[5].astype(jnp.bfloat16), "dp", axis=1, tiled=True).astype(
            jnp.float32
        ),
        lax.all_gather(shares[6].astype(jnp.bfloat16), "dp", axis=0, tiled=True).astype(
            jnp.float32
        ),
        lax.all_gather(shares[7].astype(jnp.bfloat16), "dp", axis=0, tiled=True).astype(
            jnp.float32
        ),
        lax.all_gather(shares[8].astype(jnp.bfloat16), "dp", axis=0, tiled=True).astype(
            jnp.float32
        ),
        lax.all_gather(shares[9].astype(jnp.bfloat16), "dp", axis=0, tiled=True).astype(
            jnp.float32
        ),
        lax.all_gather(shares[10].astype(jnp.bfloat16), "dp", axis=0, tiled=True).astype(
            jnp.float32
        ),
    )
    return (
        output,
        grad_x,
        whole_grads[7],
        whole_grads[8],
        whole_grads[9],
        whole_grads[10],
        whole_grads[0],
        whole_grads[1],
        whole_grads[2],
        whole_grads[6],
        whole_grads[3],
        whole_grads[4],
        whole_grads[5],
        whole_grads[6],
    )


def solution(mesh):
    placed = (
        P("dp", None),
        P("dp"),
        P(),
        P(),
        P(),
        P(),
        P(None, "tensor", None),
        P("tensor", None),
        P("tensor", None, None),
        P(),
        P(None, "tensor"),
        P("tensor"),
        P("tensor", None),
        P(),
        P("dp", None),
    )
    return jax.shard_map(
        body,
        mesh=mesh,
        in_specs=placed,
        out_specs=(
            P("dp", None),
            P("dp", None),
            P(),
            P(),
            P(),
            P(),
            P(None, "tensor", None),
            P("tensor", None),
            P("tensor", None, None),
            P(),
            P(None, "tensor"),
            P("tensor"),
            P("tensor", None),
            P(),
        ),
        check_vma=False,
    )
```

profile of v0, /device:TPU:1, one launch (start us, length us, event | category | flops | bytes accessed | tf_op | source)
XLA Modules:
  0.0 1356.6 jit_solution(9484674918558623280)
XLA Ops:
  9.0 1.7 fusion.53
  10.7 1.3 convert_reduce_fusion.1
  12.0 1.5 fusion.35
  13.5 4.4 fusion.88
  20.9 2.2 fusion.89
  24.4 2.0 fusion.50
  28.0 1.9 multiply_reduce_fusion
  29.9 2.6 multiply_convert_fusion
  35.5 1.5 convolution_add_fusion
  37.0 8.9 convert_reduce_fusion
  46.7 1.4 fusion.90
  48.1 1.4 fusion.91
  51.0 1.5 fusion.41
  53.2 1.7 bitcast_reduce_fusion
  54.9 1.4 fusion.34
  56.3 1.8 add_convert_fusion.1
  58.3 5.3 fusion.51
  63.9 3.5 fusion.55
  68.7 5.3 all-reduce.21
  74.0 370.5 %all-reduce.28 = (bf16[768]{0:T(1024)(128)(2,1)}, bf16[768]{0:T(1024)(128)(2,1)}, bf16[768]{0:T(1024)(128)(2,1)}, bf16[768]{0:T(1024)(128)(2,1)}, bf16[768,6,192...) all-reduce(bf16[768]{0:T(1024)(128)(2,1)S(1)} %get-tuple-element.14, ...), channel_id=2, replica_groups=mesh['dp'=64,'tensor'=2] {'dp'}, use_global_device_ids=true, to_apply=%region_15.16.clone | all-reduce | flops 1186176 | bytes 7110912
  446.1 5.3 fusion.75
  451.4 3.6 fusion.92
  455.1 196.1 %fusion.81 = (f32[16,1536]{1,0:T(8,128)S(1)}, f32[1536,16]{0,1:T(8,128)S(1)}) fusion(f32[768,1536]{1,0:T(8,128)} %fusion.75, f32[1536,768]{0,1:T(8,128)} %fusion.92), kind=kCustom, calls=%all-reduce-scatter.2 | all-reduce-scatter fusion | flops 3145729 | bytes 9634304
  651.2 1.3 collective-permute-start.31
  652.5 8.6 collective-permute-start.30
  661.1 1.3 collective-permute-start.29
  662.4 1.3 collective-permute-start.28
  663.7 1.3 collective-permute-start.27
  665.0 1.3 collective-permute-start.26
  666.3 6.8 collective-permute-start.25
  673.1 1.3 collective-permute-start.24
  674.4 1.6 collective-permute-start.23
  676.1 3.1 collective-permute-start.22
  679.2 3.5 collective-permute-start.21
  682.7 2.5 collective-permute-start.20
  685.2 4.0 collective-permute-start.19
  689.2 3.5 collective-permute-start.18
  692.6 2.2 collective-permute-start.17
  694.9 1.9 collective-permute-start.16
  698.1 24.8 %concatenate.28 = bf16[1536,268]{0,1:T(8,128)(2,1)} concatenate(bf16[1536,12]{0,1:T(8,128)(2,1)S(1)} %collective-permute-done.31, bf16[1536,16]{0,1:T(8,128)(2,1)S(1)} %collective-permute-done.30, bf16[1536,16]{0,1:T(8,128)(2,1)S(1)} %collective-permute-done.29, bf16[1536,16]{0,1:T(8,128)(2,1)} %copy-done.23, bf16[1536,16]{0,1:T(8,128)(2,1)} %copy-done.24, ...), dimensions={1} | concatenate | bytes 1695744
  722.9 1.5 fusion.64
  724.6 3.2 collective-permute-start.15
  727.7 4.8 collective-permute-start.14
  736.4 4.9 collective-permute-start.10
  742.7 3.2 collective-permute-start.8
  745.9 1.6 collective-permute-start.7
  747.5 1.3 collective-permute-start.6
  748.8 4.2 collective-permute-start.5
  753.0 2.8 collective-permute-start.4
  755.9 4.0 collective-permute-start.3
  760.0 2.8 collective-permute-start.2
  762.7 2.5 collective-permute-start.1
  765.3 2.2 collective-permute-start
  768.8 24.7 %concatenate.27 = bf16[268,1536]{1,0:T(8,128)(2,1)} concatenate(bf16[12,1536]{1,0:T(8,128)(2,1)S(1)} %collective-permute-done.15, bf16[16,1536]{1,0:T(8,128)(2,1)S(1)} %collective-permute-done.14, bf16[16,1536]{1,0:T(8,128)(2,1)S(1)} %collective-permute-done.13, bf16[16,1536]{1,0:T(8,128)(2,1)S(1)} %collective-permute-done.12, bf16[16,1536]{1,0:T(8,128)(2,1)S(1)} %collective-permute-done.11, ...), dimensions={0} | concatenate | bytes 1695744
  793.5 1.5 fusion.63
  801.4 316.3 %all-reduce.20 = (bf16[768]{0:T(1024)(128)(2,1)S(1)}, bf16[768]{0:T(1024)(128)(2,1)S(1)}, bf16[768]{0:T(1024)(128)(2,1)S(1)}, bf16[768]{0:T(1024)(128)(2,1)S(1)}...) all-reduce(bf16[768]{0:T(1024)(128)(2,1)S(1)} %dynamic-update-slice, ...), channel_id=1, replica_groups=mesh['dp'=64,'tensor'=2] {'dp'}, use_global_device_ids=true, to_apply=%add | all-reduce | flops 5376 | bytes 21504
  1121.4 96.1 %all-gather = bf16[64,3,6]{2,1,0:T(4,128)(2,1)S(1)} all-gather(bf16[1,3,6]{2,1,0:T(4,128)(2,1)S(1)} %fusion.68), channel_id=1, replica_groups=mesh['dp'=64,'tensor'=2] {'dp'}, dimensions={0}, use_global_device_ids=true | all-gather | bytes 2340 | tf_op jit(solution)/shard_map/all_gather | solution.py:226
  1219.3 99.8 %all_gather.39 = bf16[6,64,768]{1,0,2:T(8,128)(2,1)} all-gather(bf16[6,64,12]{1,0,2:T(8,128)(2,1)S(1)} %copy.72), channel_id=1, replica_groups=mesh['dp'=64,'tensor'=2] {'dp'}, dimensions={2}, use_global_device_ids=true | all-gather | bytes 599040 | tf_op jit(solution)/shard_map/all_gather | solution.py:229
  1319.2 2.8 copy.74
  1322.6 2.4 fusion.40
  1326.4 5.1 copy.73
  1331.5 5.2 reshape.320
  1336.7 6.0 copy.75
  1342.8 5.2 reshape.306
  (236 shorter events, 34.1 us)
Async XLA Ops:
  8.0 29.0 %copy-start = (bf16[1536,768]{1,0:T(8,128)(2,1)S(1)}, bf16[1536,768]{1,0:T(8,128)(2,1)}, u32[]{:S(2)}) copy-start(bf16[1536,768]{1,0:T(8,128)(2,1)} %param.27) | copy-start | bytes 7077892
  8.0 1314.6 %all-reduce.27.cloned.1.call-start = ((), (), s32[]{:S(2)}) async-start(), calls=%async_computation.3 | async-start | bytes 3145728 | tf_op jit(solution)/shard_map/psum | solution.py:134
  13.5 4.4 copy-start.40
  18.9 4.2 copy-start.11
  18.9 4.2 copy-start.13
  27.2 2.7 copy-start.4
  29.9 2.7 copy-start.22
  50.9 3.9 copy-start.9
  58.2 1268.2 %all-gather.7.cloned.1.call-start = ((), (), s32[]{:S(2)}) async-start(), calls=%async_computation | async-start | bytes 3194880 | tf_op jit(solution)/shard_map/all_gather | solution.py:223
  58.2 5.3 copy-start.10
  63.5 3.9 copy-start.47
  63.5 10.4 copy-start.42
  73.9 372.1 %copy-start.46 = (f32[768]{0:T(1024)S(1)}, f32[768]{0:T(1024)}, u32[]{:S(2)}) copy-start(f32[768]{0:T(1024)} %param.19) | copy-start | bytes 9220
  74.0 372.1 %copy-start.57 = (f32[768]{0:T(1024)S(1)}, f32[768]{0:T(1024)}, u32[]{:S(2)}) copy-start(f32[768]{0:T(1024)} %param.20) | copy-start | bytes 9220
  446.0 885.5 %all-gather.11.cloned.1.call-start = ((), (), s32[]{:S(2)}) async-start(), calls=%async_computation.2 | async-start | bytes 3194880 | tf_op jit(solution)/shard_map/all_gather | solution.py:238
  446.1 5.4 copy-start.3
  446.1 5.4 copy-start.6
  651.2 13.8 %collective-permute-start.31 = (bf16[1536,12]{0,1:T(8,128)(2,1)S(1)}, bf16[1536,12]{0,1:T(8,128)(2,1)S(1)}, u32[]{:S(2)}, u32[]{:S(2)}) collective-permute-start(bf16[1536,12]{0,1:T(8,128)(2,1)S(1)} %slice.115), channel_id=1, source_target_pairs={{0,32},{2,34},{4,36},{6,38},{8,40},{10,42},{12,44},{14,46},{16,48}... | collective-permute-start | bytes 110600
  652.5 13.8 %collective-permute-start.30 = (bf16[1536,16]{0,1:T(8,128)(2,1)S(1)}, bf16[1536,16]{0,1:T(8,128)(2,1)S(1)}, u32[]{:S(2)}, u32[]{:S(2)}) collective-permute-start(bf16[1536,16]{0,1:T(8,128)(2,1)S(1)} %convert.90), channel_id=1, source_target_pairs={{0,30},{2,32},{4,34},{6,36},{8,38},{10,40},{12,42},{14,44},{16,46}... | collective-permute-start | bytes 147464
  661.1 12.0 collective-permute-start.29
  662.4 12.0 collective-permute-start.28
  663.7 12.4 collective-permute-start.27
  665.0 14.2 %collective-permute-start.26 = (bf16[1536,16]{0,1:T(8,128)(2,1)S(1)}, bf16[1536,16]{0,1:T(8,128)(2,1)S(1)}, u32[]{:S(2)}, u32[]{:S(2)}) collective-permute-start(bf16[1536,16]{0,1:T(8,128)(2,1)S(1)} %convert.90), channel_id=1, source_target_pairs={{0,22},{2,24},{4,26},{6,28},{8,30},{10,32},{12,34},{14,36},{16,38}... | collective-permute-start | bytes 147464
  666.3 16.4 %collective-permute-start.25 = (bf16[1536,16]{0,1:T(8,128)(2,1)S(1)}, bf16[1536,16]{0,1:T(8,128)(2,1)S(1)}, u32[]{:S(2)}, u32[]{:S(2)}) collective-permute-start(bf16[1536,16]{0,1:T(8,128)(2,1)S(1)} %convert.90), channel_id=1, source_target_pairs={{0,20},{2,22},{4,24},{6,26},{8,28},{10,30},{12,32},{14,34},{16,36}... | collective-permute-start | bytes 147464
  673.1 12.1 collective-permute-start.24
  674.4 22.4 %copy-start.23 = (bf16[1536,16]{0,1:T(8,128)(2,1)}, bf16[1536,16]{0,1:T(8,128)(2,1)S(1)}, u32[]{:S(2)}) copy-start(bf16[1536,16]{0,1:T(8,128)(2,1)S(1)} %collective-permute-done.28) | copy-start | bytes 147460
  674.4 14.7 %collective-permute-start.23 = (bf16[1536,16]{0,1:T(8,128)(2,1)S(1)}, bf16[1536,16]{0,1:T(8,128)(2,1)S(1)}, u32[]{:S(2)}, u32[]{:S(2)}) collective-permute-start(bf16[1536,16]{0,1:T(8,128)(2,1)S(1)} %convert.90), channel_id=1, source_target_pairs={{0,16},{2,18},{4,20},{6,22},{8,24},{10,26},{12,28},{14,30},{16,32}... | collective-permute-start | bytes 147464
  676.1 20.7 %copy-start.24 = (bf16[1536,16]{0,1:T(8,128)(2,1)}, bf16[1536,16]{0,1:T(8,128)(2,1)S(1)}, u32[]{:S(2)}) copy-start(bf16[1536,16]{0,1:T(8,128)(2,1)S(1)} %collective-permute-done.27) | copy-start | bytes 147460
  676.1 16.6 %collective-permute-start.22 = (bf16[1536,16]{0,1:T(8,128)(2,1)S(1)}, bf16[1536,16]{0,1:T(8,128)(2,1)S(1)}, u32[]{:S(2)}, u32[]{:S(2)}) collective-permute-start(bf16[1536,16]{0,1:T(8,128)(2,1)S(1)} %convert.90), channel_id=1, source_target_pairs={{0,14},{2,16},{4,18},{6,20},{8,22},{10,24},{12,26},{14,28},{16,30}... | collective-permute-start | bytes 147464
  679.2 17.6 %copy-start.25 = (bf16[1536,16]{0,1:T(8,128)(2,1)}, bf16[1536,16]{0,1:T(8,128)(2,1)S(1)}, u32[]{:S(2)}) copy-start(bf16[1536,16]{0,1:T(8,128)(2,1)S(1)} %collective-permute-done.26) | copy-start | bytes 147460
  679.2 15.7 %collective-permute-start.21 = (bf16[1536,16]{0,1:T(8,128)(2,1)S(1)}, bf16[1536,16]{0,1:T(8,128)(2,1)S(1)}, u32[]{:S(2)}, u32[]{:S(2)}) collective-permute-start(bf16[1536,16]{0,1:T(8,128)(2,1)S(1)} %convert.90), channel_id=1, source_target_pairs={{0,12},{2,14},{4,16},{6,18},{8,20},{10,22},{12,24},{14,26},{16,28}... | collective-permute-start | bytes 147464
  682.7 14.2 %copy-start.26 = (bf16[1536,16]{0,1:T(8,128)(2,1)}, bf16[1536,16]{0,1:T(8,128)(2,1)S(1)}, u32[]{:S(2)}) copy-start(bf16[1536,16]{0,1:T(8,128)(2,1)S(1)} %collective-permute-done.25) | copy-start | bytes 147460
  682.7 14.8 %collective-permute-start.20 = (bf16[1536,16]{0,1:T(8,128)(2,1)S(1)}, bf16[1536,16]{0,1:T(8,128)(2,1)}, u32[]{:S(2)}, u32[]{:S(2)}) collective-permute-start(bf16[1536,16]{0,1:T(8,128)(2,1)S(1)} %convert.90), channel_id=1, source_target_pairs={{0,10},{2,12},{4,14},{6,16},{8,18},{10,20},{12,22},{14,24},{16,26}... | collective-permute-start | bytes 147464
  685.1 11.7 copy-start.27
  685.2 12.4 collective-permute-start.19
  689.1 7.7 copy-start.29
  689.2 8.4 collective-permute-start.18
  692.6 4.2 copy-start.31
  692.6 4.9 collective-permute-start.17
  694.9 3.2 collective-permute-start.16
  724.5 618.3 %all-gather.9.cloned.1.call-start = ((), (), s32[]{:S(2)}) async-start(), calls=%async_computation.1 | async-start | bytes 3194880 | tf_op jit(solution)/shard_map/all_gather | solution.py:232
  724.6 11.8 collective-permute-start.15
  727.7 13.6 %collective-permute-start.14 = (bf16[16,1536]{1,0:T(8,128)(2,1)S(1)}, bf16[16,1536]{1,0:T(8,128)(2,1)S(1)}, u32[]{:S(2)}, u32[]{:S(2)}) collective-permute-start(bf16[16,1536]{1,0:T(8,128)(2,1)S(1)} %convert.91), channel_id=1, source_target_pairs={{0,30},{2,32},{4,34},{6,36},{8,38},{10,40},{12,42},{14,44},{16,46}... | collective-permute-start | bytes 147464
  732.5 10.2 collective-permute-start.13
  733.8 12.0 collective-permute-start.12
  735.1 12.4 collective-permute-start.11
  736.4 12.4 collective-permute-start.10
  741.4 11.7 collective-permute-start.9
  742.7 13.2 collective-permute-start.8
  745.9 14.1 %collective-permute-start.7 = (bf16[16,1536]{1,0:T(8,128)(2,1)S(1)}, bf16[16,1536]{1,0:T(8,128)(2,1)S(1)}, u32[]{:S(2)}, u32[]{:S(2)}) collective-permute-start(bf16[16,1536]{1,0:T(8,128)(2,1)S(1)} %convert.91), channel_id=1, source_target_pairs={{0,16},{2,18},{4,20},{6,22},{8,24},{10,26},{12,28},{14,30},{16,32}... | collective-permute-start | bytes 147464
  747.5 15.2 %collective-permute-start.6 = (bf16[16,1536]{1,0:T(8,128)(2,1)S(1)}, bf16[16,1536]{1,0:T(8,128)(2,1)S(1)}, u32[]{:S(2)}, u32[]{:S(2)}) collective-permute-start(bf16[16,1536]{1,0:T(8,128)(2,1)S(1)} %convert.91), channel_id=1, source_target_pairs={{0,14},{2,16},{4,18},{6,20},{8,22},{10,24},{12,26},{14,28},{16,30}... | collective-permute-start | bytes 147464
  748.8 16.5 %collective-permute-start.5 = (bf16[16,1536]{1,0:T(8,128)(2,1)S(1)}, bf16[16,1536]{1,0:T(8,128)(2,1)S(1)}, u32[]{:S(2)}, u32[]{:S(2)}) collective-permute-start(bf16[16,1536]{1,0:T(8,128)(2,1)S(1)} %convert.91), channel_id=1, source_target_pairs={{0,12},{2,14},{4,16},{6,18},{8,20},{10,22},{12,24},{14,26},{16,28}... | collective-permute-start | bytes 147464
  753.0 14.6 %copy-start.28 = (bf16[16,1536]{1,0:T(8,128)(2,1)}, bf16[16,1536]{1,0:T(8,128)(2,1)S(1)}, u32[]{:S(2)}) copy-start(bf16[16,1536]{1,0:T(8,128)(2,1)S(1)} %collective-permute-done.9) | copy-start | bytes 147460
  753.0 14.5 %collective-permute-start.4 = (bf16[16,1536]{1,0:T(8,128)(2,1)S(1)}, bf16[16,1536]{1,0:T(8,128)(2,1)S(1)}, u32[]{:S(2)}, u32[]{:S(2)}) collective-permute-start(bf16[16,1536]{1,0:T(8,128)(2,1)S(1)} %convert.91), channel_id=1, source_target_pairs={{0,10},{2,12},{4,14},{6,16},{8,18},{10,20},{12,22},{14,24},{16,26}... | collective-permute-start | bytes 147464
  755.9 11.7 copy-start.30
  755.9 11.6 collective-permute-start.3
  759.9 7.7 copy-start.32
  760.0 7.6 collective-permute-start.2
  762.7 4.9 copy-start.34
  762.7 4.8 collective-permute-start.1
  765.3 3.5 collective-permute-start
  1217.8 104.8 %copy-start.48 = (f32[768]{0:T(1024)S(1)}, f32[768]{0:T(1024)}, u32[]{:S(2)}) copy-start(f32[768]{0:T(1024)} %param.28) | copy-start | bytes 9220
  1217.8 104.8 %copy-start.49 = (f32[768]{0:T(1024)S(1)}, f32[768]{0:T(1024)}, u32[]{:S(2)}) copy-start(f32[768]{0:T(1024)} %param.24) | copy-start | bytes 9220
  1322.0 25.9 %copy-start.43 = (f32[768]{0:T(1024)}, f32[768]{0:T(1024)S(1)}, u32[]{:S(2)}) copy-start(f32[768]{0:T(1024)S(1)} %convert_element_type.231) | copy-start | bytes 9220
  (31 other events, 50.6 us)
Sparse Core Ops, SparseCore 0:
  58.3 67.3 all-reduce.26
Sparse Core Ops, SparseCore 1:
  446.1 79.1 all-gather.6
  724.6 69.3 all-gather.10
  797.5 67.3 all-gather.8
where the time goes:
time: 1370 us; the launch traced here: 1360 us
  blocking collectives  1080 us (79%)
  local copies, waits for them, and re-layouts  92.1 us (7%)
  starting transfers between devices  88.2 us (6%)
  matrix products  47.9 us (3%)
  other arithmetic  22.5 us (2%)
  between operations  21.3 us (2%)
    unnamed x3, blocking collectives  883 us
    all_gather x1, blocking collectives, body(): lax.all_gather(shares[2].astype(jnp.bfloat16), 'dp', axis=2, tiled=True)  99.8 us
    all_gather x1, blocking collectives, body(): lax.all_gather(shares[1].astype(jnp.bfloat16), 'dp', axis=1, tiled=True)  96.1 us
    unnamed x32, starting transfers between devices  88 us
    unnamed x150, local copies, waits for them, and re-layouts  78 us
  transfers between devices with their start and end apart: 36, of which 1 were waited for; matrix products, arithmetic and copies ran while one was open for 22% of the time, Pallas kernels for 0%

commit v1 on v0

v1 whole, which is shorter than its diff:
```python
import functools

import jax
import jax.numpy as jnp
import numpy as np
from jax import lax
from jax.experimental import pallas as pl
from jax.experimental.pallas import tpu as pltpu
from jax.sharding import PartitionSpec as P

HD = 64
ROT = 16
SEQ = 512
D = 768
FFL = 1536
EPS = 1e-05
MASKED = -1000000000.0
BF = jnp.bfloat16
F32 = jnp.float32


def place(z, x, y, c):
    return ((z * 4 + x) * 4 + y) * 2 + c


def build_perm(kind, step=1):
    pairs = []
    for z in range(2):
        for x in range(4):
            for y in range(4):
                for c in range(2):
                    if kind == "core":
                        dst = place(z, x, y, 1 - c)
                    elif kind == "z":
                        dst = place(1 - z, x, y, c)
                    elif (kind == "first") == (c == 0):
                        dst = place(z, (x + step) % 4, y, c)
                    else:
                        dst = place(z, x, (y + step) % 4, c)
                    pairs.append((place(z, x, y, c), dst))
    return pairs


CORE = build_perm("core")
ZHI = build_perm("z")
FIRST = {d: build_perm("first", d) for d in (1, 2, 3)}
SECOND = {d: build_perm("second", d) for d in (1, 2, 3)}
SWAP = [(0, 1), (1, 0)]


def move(v, perm):
    return lax.ppermute(v, "dp", perm)


def dot(a, b):
    return jnp.dot(a, b, preferred_element_type=F32)


def dot_nt(a, b):
    return lax.dot_general(a, b, (((1,), (1,)), ((), ())), preferred_element_type=F32)


def dot_tn(a, b):
    return lax.dot_general(a, b, (((0,), (0,)), ((), ())), preferred_element_type=F32)


def norm_parts(x):
    xf = x.astype(F32)
    centred = xf - jnp.mean(xf, axis=-1, keepdims=True)
    rstd = lax.rsqrt(jnp.mean(centred * centred, axis=-1, keepdims=True) + EPS)
    return centred * rstd, rstd


def mlp_kernel(first, half_ref, *refs):
    if first:
        (x_ref, cot_ref, vec_ref, bfc_ref, wfc_ref, wproj_ref,
         gw_ref, gm_ref, mo_ref, gb_ref, normed, gy) = refs
    else:
        (x_ref, cot_ref, vec_ref, bfc_ref, wfc_ref, wproj_ref, gm_in, mo_in,
         gw_ref, gm_ref, mo_ref, gb_ref, normed, gy) = refs
    i = pl.program_id(0)

    @pl.when(i == 0)
    def _():
        n, _unused = norm_parts(x_ref[...])
        normed[...] = (n * vec_ref[2:3, :] + vec_ref[3:4, :]).astype(BF)
        gy[...] = cot_ref[...].astype(BF)
        if first:
            gm_ref[...] = jnp.zeros_like(gm_ref)
            mo_ref[...] = jnp.zeros_like(mo_ref)
        else:
            gm_ref[...] = gm_in[...]
            mo_ref[...] = mo_in[...]

    wfc = wfc_ref[...]
    wproj = wproj_ref[...]
    hidden = dot(normed[...], wfc) + bfc_ref[...]
    cdf = 0.5 * (1.0 + lax.erf(hidden * np.float32(np.sqrt(0.5))))
    pdf = jnp.exp(-0.5 * hidden * hidden) * np.float32(1.0 / np.sqrt(2.0 * np.pi))
    act = (hidden * cdf).astype(BF)
    slope = cdf + hidden * pdf
    ghid = (dot_nt(gy[...], wproj) * slope).astype(BF)
    gb_ref[...] = jnp.sum(ghid.astype(F32), axis=0, keepdims=True)
    at = pl.multiple_of(i * 256, 256)
    gw_ref[0, pl.ds(at, 256), :] = dot_tn(act, gy[...]).astype(BF)
    gw_ref[1, :, pl.ds(at, 256)] = dot_tn(normed[...], ghid).astype(BF)
    gm_ref[...] += dot_nt(ghid, wfc)
    mo_ref[...] += dot(act, wproj)


def whole(shape):
    return pl.BlockSpec(shape, lambda *_: (0,) * len(shape))


def mlp_half(half, x, cot, vec, bfc, wfc, wproj, carry=None):
    tok = (SEQ, D)
    in_specs = [
        whole(tok), whole(tok), whole((8, D)),
        pl.BlockSpec((1, 256), lambda i, h: (0, h[0] * 3 + i)),
        pl.BlockSpec((D, 256), lambda i, h: (0, h[0] * 3 + i)),
        pl.BlockSpec((256, D), lambda i, h: (h[0] * 3 + i, 0)),
    ]
    args = [x, cot, vec, bfc, wfc, wproj]
    if carry is not None:
        in_specs += [whole(tok), whole(tok)]
        args += list(carry)
    return pl.pallas_call(
        functools.partial(mlp_kernel, carry is None),
        grid_spec=pltpu.PrefetchScalarGridSpec(
            num_scalar_prefetch=1,
            grid=(3,),
            in_specs=in_specs,
            out_specs=[
                whole((2, D, D)), whole(tok), whole(tok),
                pl.BlockSpec((1, 256), lambda i, h: (0, i)),
            ],
            scratch_shapes=[pltpu.VMEM(tok, BF), pltpu.VMEM(tok, BF)],
        ),
        out_shape=[
            jax.ShapeDtypeStruct((2, D, D), BF),
            jax.ShapeDtypeStruct(tok, F32),
            jax.ShapeDtypeStruct(tok, F32),
            jax.ShapeDtypeStruct((1, D), F32),
        ],
        compiler_params=pltpu.CompilerParams(
            dimension_semantics=("arbitrary",), vmem_limit_bytes=36 << 20
        ),
        cost_estimate=pl.CostEstimate(
            flops=6 * 2 * SEQ * D * D, bytes_accessed=14 << 20, transcendentals=2 * SEQ * D
        ),
        name="mlp_send" if carry is None else "mlp_keep",
    )(half, *args)


def attend_kernel(
    half_ref, x_ref, cot_ref, vec_ref, seg_ref, freq_ref, wq_ref, bq_ref, wo_ref,
    gm_ref, mo_ref, gb1_ref, gb2_ref,
    grads_ref, n1_ref, gy_ref, out_ref, gx_ref, sm_ref,
    bias, ctab, s1tab, s2tab, gn1, acc,
):
    p = pl.program_id(0)
    lane = lax.broadcasted_iota(jnp.int32, (1, 128), 1)

    @pl.when(p == 0)
    def _():
        n, _unused = norm_parts(x_ref[...])
        n1_ref[...] = (n * vec_ref[0:1, :] + vec_ref[1:2, :]).astype(BF)
        gy_ref[...] = cot_ref[...].astype(BF)
        seg_row = seg_ref[...]
        seg_col = jnp.transpose(jnp.broadcast_to(seg_row, (128, SEQ)))
        row_at = lax.broadcasted_iota(jnp.int32, (SEQ, 128), 0)
        before = jnp.zeros((SEQ, 128), F32)
        for b in range(SEQ // 128):
            seg_k = seg_row[:, b * 128 : (b + 1) * 128]
            before += jnp.where(seg_k < seg_col, 1.0, 0.0)
            k_at = lane + b * 128
            ok = (seg_k == seg_col) & (row_at >= k_at)
            bias[:, b * 128 : (b + 1) * 128] = jnp.where(ok, 0.0, MASKED)
        opening = jnp.sum(before, axis=1, keepdims=True)
        offset = row_at.astype(F32) - opening
        angle = offset * freq_ref[...]
        cosine, sine = jnp.cos(angle), jnp.sin(angle)
        j = lax.rem(lane, 64)
        ctab[...] = jnp.where(j < 16, cosine, 1.0)
        s1tab[...] = jnp.where(j < 8, -sine, 0.0)
        s2tab[...] = jnp.where((j >= 8) & (j < 16), sine, 0.0)
        gn1[...] = jnp.zeros_like(gn1)
        acc[...] = mo_ref[...]

    def rot(u, sign):
        turned = pltpu.roll(u, 120, 1) * s1tab[...] + pltpu.roll(u, 8, 1) * s2tab[...]
        return u * ctab[...] + sign * turned

    def rows(h, part):
        at = h * 192 + part * 64
        return wq_ref[at : at + 64, :]

    wp = jnp.concatenate([rows(h, part) for part in range(3) for h in range(2)], axis=0)
    n1 = n1_ref[...]
    mixed = dot_nt(n1, wp) + bq_ref[0]
    q = rot(mixed[:, :128], 1.0).astype(BF) * 0.125
    k = rot(mixed[:, 128:256], 1.0).astype(BF)
    v = mixed[:, 256:].astype(BF)
    wo = wo_ref[...]
    go = dot_nt(gy_ref[...], wo).astype(BF)
    zero = jnp.zeros((), BF)
    half_len = SEQ // 2
    ctx = [None, None]
    gq = [None, None]
    gk = [None, None]
    gv = [None, None]

    def add(slot, i, val):
        slot[i] = val if slot[i] is None else slot[i] + val

    for hh in range(2):
        mine = (lane // 64) == hh
        qm = jnp.where(mine, q, zero)
        km = jnp.where(mine, k, zero)
        vm = jnp.where(mine, v, zero)
        gom = jnp.where(mine, go, zero)
        for b in range(2):
            r = slice(b * half_len, (b + 1) * half_len)
            end = (b + 1) * half_len
            s = dot_nt(qm[r], k[:end]) + bias[r, :end]
            powers = jnp.exp(s - jnp.max(s, axis=-1, keepdims=True))
            probs = powers * (1.0 / jnp.sum(powers, axis=-1, keepdims=True))
            weights = probs.astype(BF)
            add(ctx, b, dot(weights, vm[:end]))
            gp = dot_nt(gom[r], v[:end])
            delta = jnp.sum(probs * gp, axis=-1, keepdims=True)
            gs = (probs * (gp - delta)).astype(BF)
            add(gq, b, dot(gs, km[:end]))
            for kb in range(b + 1):
                kr = slice(kb * half_len, (kb + 1) * half_len)
                add(gk, kb, dot_tn(gs[:, kr], qm[r]))
                add(gv, kb, dot_tn(weights[:, kr], gom[r]))
    ctx_all = jnp.concatenate(ctx, axis=0).astype(BF)
    gq_all = rot(jnp.concatenate(gq, axis=0) * 0.125, -1.0).astype(BF)
    gk_all = rot(jnp.concatenate(gk, axis=0), -1.0).astype(BF)
    gv_all = jnp.concatenate(gv, axis=0).astype(BF)
    parts = (gq_all, gk_all, gv_all)
    gmix = jnp.concatenate(parts, axis=1)
    gn1[...] += dot(gmix, wp)
    acc[...] += dot(ctx_all, wo)
    spots = ((0, 128, 256, 640), (384, 512, 768, 1280), (896, 1024, 1152, 1408))
    for step in range(3):

        @pl.when(p == step)
        def _(step=step):
            for at, val in zip(spots[step], parts + (ctx_all,)):
                grads_ref[:, at : at + 128] = val
            for part in range(3):
                row = 42 + step * 3 + part
                sm_ref[row : row + 1, :] = jnp.sum(
                    parts[part].astype(F32), axis=0, keepdims=True
                )

    @pl.when(p == 2)
    def _():
        out_ref[...] = acc[...].astype(BF)
        n, rstd = norm_parts(x_ref[...])
        u1, u2 = gn1[...], gm_ref[...]
        ug = u1 * vec_ref[0:1, :] + u2 * vec_ref[2:3, :]
        m1 = jnp.mean(ug, axis=-1, keepdims=True)
        m2 = jnp.mean(ug * n, axis=-1, keepdims=True)
        gx_ref[...] = ((ug - m1 - n * m2) * rstd).astype(BF)

        def put(row, vec):
            for j in range(6):
                sm_ref[pl.ds(row + j, 1), :] = vec[:, j * 128 : (j + 1) * 128]

        put(0, jnp.sum(u1 * n, axis=0, keepdims=True))
        put(6, jnp.sum(u1, axis=0, keepdims=True))
        put(12, jnp.sum(u2 * n, axis=0, keepdims=True))
        put(18, jnp.sum(u2, axis=0, keepdims=True))
        put(24, jnp.sum(cot_ref[...], axis=0, keepdims=True))
        put(30 + 6 * half_ref[0], gb1_ref[...])
        put(30 + 6 * (1 - half_ref[0]), gb2_ref[...])
        sm_ref[51:64, :] = jnp.zeros((13, 128), F32)


def attend(half, x, cot, vec, seg, freq, wq, bq, wo, gm, mo, gb1, gb2):
    tok = (SEQ, D)
    return pl.pallas_call(
        attend_kernel,
        grid_spec=pltpu.PrefetchScalarGridSpec(
            num_scalar_prefetch=1,
            grid=(3,),
            in_specs=[
                whole(tok), whole(tok), whole((8, D)), whole((1, SEQ)), whole((1, 128)),
                pl.BlockSpec((384, D), lambda p, h: (p, 0)),
                pl.BlockSpec((1, 1, 384), lambda p, h: (p, 0, 0)),
                pl.BlockSpec((128, D), lambda p, h: (p, 0)),
                whole(tok), whole(tok), whole((1, D)), whole((1, D)),
            ],
            out_specs=[
                whole((SEQ, 1536)), whole(tok), whole(tok), whole(tok), whole(tok),
                whole((64, 128)),
            ],
            scratch_shapes=[
                pltpu.VMEM((SEQ, SEQ), F32),
                pltpu.VMEM((SEQ, 128), F32),
                pltpu.VMEM((SEQ, 128), F32),
                pltpu.VMEM((SEQ, 128), F32),
                pltpu.VMEM(tok, F32),
                pltpu.VMEM(tok, F32),
            ],
        ),
        out_shape=[
            jax.ShapeDtypeStruct((SEQ, 1536), BF),
            jax.ShapeDtypeStruct(tok, BF),
            jax.ShapeDtypeStruct(tok, BF),
            jax.ShapeDtypeStruct(tok, BF),
            jax.ShapeDtypeStruct(tok, BF),
            jax.ShapeDtypeStruct((64, 128), F32),
        ],
        compiler_params=pltpu.CompilerParams(
            dimension_semantics=("arbitrary",), vmem_limit_bytes=48 << 20
        ),
        cost_estimate=pl.CostEstimate(
            flops=14 << 30, bytes_accessed=16 << 20, transcendentals=2 << 20
        ),
        name="attend",
    )(half, x, cot, vec, seg, freq, wq, bq, wo, gm, mo, gb1, gb2)


def wgrad_kernel(half_ref, g_ref, n1_ref, gy_ref, o_ref):
    i = pl.program_id(0)
    is_ctx = i >= 5 - half_ref[0]

    @pl.when(is_ctx)
    def _():
        o_ref[...] = dot_tn(g_ref[...], gy_ref[...]).astype(BF)

    @pl.when(jnp.logical_not(is_ctx))
    def _():
        o_ref[...] = dot_tn(g_ref[...], n1_ref[...]).astype(BF)


def wgrad_half(half, grads, n1, gy, name):
    tok = (SEQ, D)
    return pl.pallas_call(
        wgrad_kernel,
        grid_spec=pltpu.PrefetchScalarGridSpec(
            num_scalar_prefetch=1,
            grid=(6,),
            in_specs=[
                pl.BlockSpec((SEQ, 128), lambda i, h: (0, h[0] * 6 + i)),
                whole(tok), whole(tok),
            ],
            out_specs=pl.BlockSpec((128, D), lambda i, h: (i, 0)),
        ),
        out_shape=jax.ShapeDtypeStruct((D, D), BF),
        compiler_params=pltpu.CompilerParams(
            dimension_semantics=("arbitrary",), vmem_limit_bytes=24 << 20
        ),
        cost_estimate=pl.CostEstimate(
            flops=2 * SEQ * D * D, bytes_accessed=4 << 20, transcendentals=0
        ),
        name=name,
    )(half, grads, n1, gy)


def pick(v, index, axis):
    return lax.dynamic_index_in_dim(v, index, axis, keepdims=False)


def reduce_chunks(total, pos):
    a1, a2, z = pos
    got = [move(total((a1 + d) % 4).astype(BF), FIRST[d]) for d in (1, 3, 2)]
    own = total(a1)
    for g in got:
        own = own + g.astype(F32)
    n, _, w = own.shape
    own = own.reshape(n, 4, 48, w)
    got = [move(pick(own, (a2 + d) % 4, 1).astype(BF), SECOND[d]) for d in (1, 3, 2)]
    own = pick(own, a2, 1)
    for g in got:
        own = own + g.astype(F32)
    own = own.reshape(n, 2, 24, w)
    got = move(pick(own, 1 - z, 1).astype(BF), ZHI)
    return pick(own, z, 1) + got.astype(F32)


def gather_chunks(mine, pos):
    a1, a2, z = pos
    n, _, w = mine.shape
    other = move(mine, ZHI)
    low = jnp.where(z == 0, mine, other)
    high = jnp.where(z == 0, other, mine)
    part = jnp.stack([low, high], axis=1).reshape(n, 48, w)
    got = {d: move(part, SECOND[d]) for d in (1, 3, 2)}
    ring = jnp.stack([part, got[3], got[2], got[1]] + [part, got[3], got[2]], axis=1)
    chunk = lax.dynamic_slice_in_dim(ring, (4 - a2) % 4, 4, 1).reshape(n, 192, w)
    got = {d: move(chunk, FIRST[d]) for d in (1, 3, 2)}
    chunks = [chunk, got[1], got[2], got[3]]
    return chunks + [move(c, CORE) for c in chunks]


def unpack_mlp_kernel(pos_ref, *refs):
    chunks, (proj_ref, fc_ref), (buf, sems) = refs[:8], refs[8:10], refs[10:]
    copies = []
    for s in range(8):
        half, j = pos_ref[2 * s], pos_ref[2 * s + 1]
        buf[s] = chunks[s][...].astype(F32)
        row = pl.multiple_of(half * 768 + j * 192, 64)
        copies.append(
            pltpu.make_async_copy(buf.at[s, 0], proj_ref.at[pl.ds(row, 192), :], sems.at[s, 0])
        )
        copies[-1].start()
        row = pl.multiple_of(j * 192, 64)
        col = pl.multiple_of(half * 768, 128)
        copies.append(
            pltpu.make_async_copy(
                buf.at[s, 1], fc_ref.at[pl.ds(row, 192), pl.ds(col, 768)], sems.at[s, 1]
            )
        )
        copies[-1].start()
    for c in copies:
        c.wait()


def unpack_mlp(pos, chunks):
    return pl.pallas_call(
        unpack_mlp_kernel,
        grid_spec=pltpu.PrefetchScalarGridSpec(
            num_scalar_prefetch=1,
            grid=(1,),
            in_specs=[whole((2, 192, D))] * 8,
            out_specs=[pl.BlockSpec(memory_space=pl.ANY)] * 2,
            scratch_shapes=[
                pltpu.VMEM((8, 2, 192, D), F32),
                pltpu.SemaphoreType.DMA((8, 2)),
            ],
        ),
        out_shape=[
            jax.ShapeDtypeStruct((FFL, D), F32),
            jax.ShapeDtypeStruct((D, FFL), F32),
        ],
        compiler_params=pltpu.CompilerParams(vmem_limit_bytes=32 << 20),
        cost_estimate=pl.CostEstimate(flops=0, bytes_accessed=14 << 20, transcendentals=0),
        name="unpack_mlp",
    )(pos, *chunks)


def block_row(half, b):
    qkv_blocks = 10 - 2 * half
    is_out = b >= qkv_blocks
    out_row = (b - qkv_blocks + 2 * half) * 64
    t = b + 10 * half
    pair, within = t // 6, t % 6
    qkv_row = (pair * 2 + within % 2) * 192 + (within // 2) * 64
    return is_out, out_row, qkv_row


def unpack_attn_kernel(pos_ref, *refs):
    chunks, (qkv_ref, out_ref, sm_ref), (buf, sems) = refs[:8], refs[8:11], refs[11:]
    copies = []
    for s in range(8):
        half, j = pos_ref[2 * s], pos_ref[2 * s + 1]
        buf[s] = chunks[s][0, :, :D].astype(F32)

        @pl.when((half == 0) & (j == 0))
        def _(s=s):
            sm_ref[...] = chunks[s][0, :64, D:].astype(F32)

        for t in range(3):
            is_out, out_row, qkv_row = block_row(half, j * 3 + t)
            src = buf.at[s, pl.ds(t * 64, 64), :]
            to_out = pltpu.make_async_copy(
                src,
                out_ref.at[pl.ds(pl.multiple_of(jnp.where(is_out, out_row, 0), 64), 64), :],
                sems.at[s, t],
            )
            to_qkv = pltpu.make_async_copy(
                src,
                qkv_ref.at[pl.ds(pl.multiple_of(jnp.where(is_out, 0, qkv_row), 64), 64), :],
                sems.at[s, t],
            )

            @pl.when(is_out)
            def _(to_out=to_out):
                to_out.start()

            @pl.when(jnp.logical_not(is_out))
            def _(to_qkv=to_qkv):
                to_qkv.start()

            copies.append((is_out, to_out, to_qkv))
    for is_out, to_out, to_qkv in copies:

        @pl.when(is_out)
        def _(to_out=to_out):
            to_out.wait()

        @pl.when(jnp.logical_not(is_out))
        def _(to_qkv=to_qkv):
            to_qkv.wait()


def unpack_attn(pos, chunks):
    return pl.pallas_call(
        unpack_attn_kernel,
        grid_spec=pltpu.PrefetchScalarGridSpec(
            num_scalar_prefetch=1,
            grid=(1,),
            in_specs=[whole((1, 192, 896))] * 8,
            out_specs=[
                pl.BlockSpec(memory_space=pl.ANY),
                pl.BlockSpec(memory_space=pl.ANY),
                whole((64, 128)),
            ],
            scratch_shapes=[
                pltpu.VMEM((8, 192, D), F32),
                pltpu.SemaphoreType.DMA((8, 3)),
            ],
        ),
        out_shape=[
            jax.ShapeDtypeStruct((1152, D), F32),
            jax.ShapeDtypeStruct((384, D), F32),
            jax.ShapeDtypeStruct((64, 128), F32),
        ],
        compiler_params=pltpu.CompilerParams(vmem_limit_bytes=24 << 20),
        cost_estimate=pl.CostEstimate(flops=0, bytes_accessed=8 << 20, transcendentals=0),
        name="unpack_attn",
    )(pos, *chunks)


def body(
    layer_input, seg_ids, ln1_gain, ln1_bias, ln2_gain, ln2_bias, w_qkv, b_qkv, w_out, b_out,
    w_fc, b_fc, w_proj, b_proj, cotangent,
):
    me = lax.axis_index("dp")
    core = me % 2
    y = (me // 2) % 4
    x = (me // 8) % 4
    z = me // 32
    a1 = jnp.where(core == 0, x, y)
    a2 = jnp.where(core == 0, y, x)
    pos = (a1, a2, z)
    table = []
    for half, first in ((core, a1), (1 - core, a2)):
        for d in range(4):
            table += [half, (first - d) % 4]
    table = jnp.stack(table).astype(jnp.int32)
    keep = core.reshape(1).astype(jnp.int32)
    send = 1 - keep

    bias_sum = b_out + b_proj
    zero = jnp.zeros_like(ln1_gain)
    vec = jnp.stack([ln1_gain, ln1_bias, ln2_gain, ln2_bias, bias_sum, zero, zero, zero])
    bfc = b_fc.reshape(1, FFL)
    wq = jnp.transpose(w_qkv, (1, 2, 0)).reshape(1152, D)
    wo = w_out.reshape(384, D)
    bq = b_qkv.reshape(3, 2, 3, 64).transpose(0, 2, 1, 3).reshape(3, 1, 384)
    seg = seg_ids.astype(F32).reshape(1, SEQ)
    freq = np.float32(10000.0) ** (np.arange(ROT // 2).astype(np.float32) * np.float32(-2.0 / ROT))
    freq = jnp.asarray(np.tile(freq, 16)[None, :].astype(np.float32))

    gw_send, gm, mo, gb_send = mlp_half(send, layer_input, cotangent, vec, bfc, w_fc, w_proj)
    gw_recv = move(gw_send, CORE).reshape(2, 4, 192, D)
    gw_keep, gm, mo, gb_keep = mlp_half(
        keep, layer_input, cotangent, vec, bfc, w_fc, w_proj, (gm, mo)
    )
    gw_keep = gw_keep.reshape(2, 4, 192, D)

    def mlp_total(j):
        return pick(gw_keep, j, 1).astype(F32) + pick(gw_recv, j, 1).astype(F32)

    mlp_mine = reduce_chunks(mlp_total, pos).astype(BF)

    grads, n1, gy, out_part, gx_part, small = attend(
        send, layer_input, cotangent, vec, seg, freq, wq, bq, wo, gm, mo, gb_send, gb_keep
    )
    norms = small[:24] + lax.ppermute(small[:24], "tensor", SWAP)
    small = jnp.concatenate([norms, small[24:]], axis=0)
    small = small + move(small, CORE)
    aw_send = wgrad_half(send, grads, n1, gy, "wgrad_send")
    aw_recv = move(aw_send, CORE).reshape(1, 4, 192, D)
    aw_keep = wgrad_half(keep, grads, n1, gy, "wgrad_keep").reshape(1, 4, 192, D)
    small_rows = jnp.pad(small, ((0, 128), (0, 0)))[None]

    def attn_total(j):
        main = pick(aw_keep, j, 1).astype(F32) + pick(aw_recv, j, 1).astype(F32)
        return jnp.concatenate([main, jnp.where(j == 0, small_rows, 0.0)], axis=2)

    attn_mine = reduce_chunks(attn_total, pos).astype(BF)

    out_other = lax.ppermute(out_part, "tensor", SWAP)
    gx_other = lax.ppermute(gx_part, "tensor", SWAP)
    output = (
        layer_input.astype(F32) + (out_part.astype(F32) + out_other.astype(F32)) + bias_sum
    ).astype(BF)
    grad_x = cotangent + (gx_part.astype(F32) + gx_other.astype(F32))

    g_proj, g_fc = unpack_mlp(table, gather_chunks(mlp_mine, pos))
    g_qkv, g_out, sm = unpack_attn(table, gather_chunks(attn_mine, pos))
    g_qkv = jnp.transpose(g_qkv.reshape(6, 192, D), (2, 0, 1))
    g_out = g_out.reshape(6, 64, D)
    vecs = [sm[6 * i : 6 * i + 6].reshape(D) for i in range(5)]
    g_bfc = sm[30:42].reshape(FFL)
    g_bqkv = sm[42:51].reshape(3, 3, 2, 64).transpose(0, 2, 1, 3).reshape(6, 192)
    return (
        output, grad_x, vecs[0], vecs[1], vecs[2], vecs[3], g_qkv, g_bqkv, g_out, vecs[4],
        g_fc, g_bfc, g_proj, vecs[4],
    )


def solution(mesh):
    placed = (
        P("dp", None), P("dp"), P(), P(), P(), P(),
        P(None, "tensor", None), P("tensor", None), P("tensor", None, None), P(),
        P(None, "tensor"), P("tensor"), P("tensor", None), P(), P("dp", None),
    )
    return jax.shard_map(
        body,
        mesh=mesh,
        in_specs=placed,
        out_specs=(
            P("dp", None), P("dp", None), P(), P(), P(), P(),
            P(None, "tensor", None), P("tensor", None), P("tensor", None, None), P(),
            P(None, "tensor"), P("tensor"), P("tensor", None), P(),
        ),
        check_vma=False,
    )
```

time: 1370 us -> 204 us (0.15)
  blocking collectives: 1080 us -> 0 us
  local copies, waits for them, and re-layouts: 92.1 us -> 19.4 us
  Pallas kernels: 0 us -> 48.8 us
  matrix products: 47.9 us -> 0 us
  waiting for transfers between devices: 0.71 us -> 41.3 us
  between operations: 21.3 us -> 1.15 us
    unnamed x3 -> x0, blocking collectives: 883 us -> none
    all_gather x2 -> x0, blocking collectives: 196 us -> none  [the longest x1 99.8 us: body(): lax.all_gather(shares[2].astype(jnp.bfloat16), 'dp', axis=2, tiled=True)]
    unnamed x32 -> x0, starting transfers between devices: 88 us -> none
    ppermute x0 -> x42, starting transfers between devices: none -> 78.9 us  [the longest x39 75.5 us: move(): return lax.ppermute(v, 'dp', perm)]
    unnamed x150 -> x71, local copies, waits for them, and re-layouts: 78 us -> 12.7 us
    pallas_call x0 -> x7, Pallas kernels: none -> 48.8 us  [the longest x1 19.7 us: attend(): pl.pallas_call(attend_kernel, grid_spec=pltpu.PrefetchScalarGridSpec(num_...]
    dot_general x18 -> x0, matrix products: 47.9 us -> none  [the longest x4 17.7 us: contract_rows(): lax.dot_general(left_mat, right_mat, (((0,), (0,)), ((), ())), preferred_...]
    ppermute x0 -> x42, waiting for transfers between devices: none -> 41.3 us  [the longest x39 40.5 us: move(): return lax.ppermute(v, 'dp', perm)]
  transfers between devices with their start and end apart: 36 -> 42, of which waited for: 1 -> 18; matrix products, arithmetic and copies ran while one was open for 22% -> 7% of each run, Pallas kernels for 0% -> 3%
where the time goes in v1:
time: 204 us; the launch traced here: 203 us
  starting transfers between devices  78.9 us (39%)
  Pallas kernels  48.8 us (24%)
  waiting for transfers between devices  41.3 us (20%)
  local copies, waits for them, and re-layouts  19.4 us (10%)
  other arithmetic  13.8 us (7%)
    ppermute x39, starting transfers between devices, move(): return lax.ppermute(v, 'dp', perm)  75.5 us
    ppermute x39, waiting for transfers between devices, move(): return lax.ppermute(v, 'dp', perm)  40.5 us
    pallas_call x1, Pallas kernels, attend(): pl.pallas_call(attend_kernel, grid_spec=pltpu.PrefetchScalarGridSpec(num_...  19.7 us
    pallas_call x2, Pallas kernels, mlp_half(): pl.pallas_call(functools.partial(mlp_kernel, carry is None), grid_spec=pl...  13.2 us
    unnamed x71, local copies, waits for them, and re-layouts  12.7 us
    pallas_call x1, Pallas kernels, unpack_mlp(): pl.pallas_call(unpack_mlp_kernel, grid_spec=pltpu.PrefetchScalarGridSpec(...  5.97 us
    pallas_call x2, Pallas kernels, wgrad_half(): pl.pallas_call(wgrad_kernel, grid_spec=pltpu.PrefetchScalarGridSpec(num_s...  5.73 us
    pallas_call x1, Pallas kernels, unpack_attn(): pl.pallas_call(unpack_attn_kernel, grid_spec=pltpu.PrefetchScalarGridSpec...  4.26 us
  transfers between devices with their start and end apart: 42, of which 18 were waited for; matrix products, arithmetic and copies ran while one was open for 7% of the time, Pallas kernels for 3%

profile of v1, /device:TPU:1, one launch (start us, length us, event | category | flops | bytes accessed | tf_op | source)
XLA Modules:
  0.0 203.3 jit_solution(4596172301934146076)
XLA Ops:
  6.4 1.4 copy-done.2
  7.8 1.1 copy-done.7
  9.0 1.7 copy-done.17
  10.6 1.7 copy-done.18
  12.3 7.1 %mlp_send.1 = (bf16[2,768,768]{2,1,0:T(8,128)(2,1)}, f32[512,768]{1,0:T(8,128)S(1)}, f32[512,768]{1,0:T(8,128)S(1)}, f32[1,768]{1,0:T(1,128)S(1)}) custom-call(s32[1]{0:T(128)S(6)} %sub.42.half_ref, bf16[512,768]{1,0:T(8,128)(2,1)S(1)} %copy-done.7, f32[512,768]{1,0:T(8,128)S(1)} %copy-done.2, f32[8,768]{1,0:T(8,128)S(1)} %stack.110.refs_2_.vec_ref, ...), custom_call_target="tpu_custom_call" | custom-call | flops 3623878656 | bytes 14680064 | tf_op jit(solution)/shard_map/mlp_send/pallas_call | solution.py:127
  19.5 6.1 %mlp_keep.1 = (bf16[2,768,768]{2,1,0:T(8,128)(2,1)S(1)}, f32[512,768]{1,0:T(8,128)S(1)}, f32[512,768]{1,0:T(8,128)S(1)}, f32[1,768]{1,0:T(1,128)S(1)}) custom-call(s32[1]{0:T(128)} %bitcast.half_ref, bf16[512,768]{1,0:T(8,128)(2,1)S(1)} %copy-done.7, f32[512,768]{1,0:T(8,128)S(1)} %copy-done.3, f32[8,768]{1,0:T(8,128)S(1)} %stack.110.refs_2_.vec_ref, ...), custom_call_target="tpu_custom_call" | custom-call | flops 3623878656 | bytes 14680064 | tf_op jit(solution)/shard_map/mlp_keep/pallas_call | solution.py:127
  25.6 1.4 copy-done
  27.0 1.1 copy-done.21
  28.1 1.1 copy-done.22
  29.2 19.7 %attend.1 = (bf16[512,1536]{1,0:T(8,128)(2,1)S(1)}, bf16[512,768]{1,0:T(8,128)(2,1)S(1)}, bf16[512,768]{1,0:T(8,128)(2,1)S(1)}, bf16[512,768]{1,0:T(8,128)(2,1)S...) custom-call(s32[1]{0:T(128)S(6)} %sub.42.half_ref, bf16[512,768]{1,0:T(8,128)(2,1)S(1)} %copy-done.8, ...), custom_call_target="tpu_custom_call" | custom-call | flops 15032385536 | bytes 16777216 | tf_op jit(solution)/shard_map/attend/pallas_call | solution.py:285
  49.0 3.5 %wgrad_send.1 = bf16[768,768]{1,0:T(8,128)(2,1)} custom-call(s32[1]{0:T(128)S(6)} %sub.42.half_ref, bf16[512,1536]{1,0:T(8,128)(2,1)S(1)} %get-tuple-element.41.g_ref, bf16[512,768]{1,0:T(8,128)(2,1)S(1)} %get-tuple-element.42.n1_ref, bf16[512,768]{1,0:T(8,128)(2,1)S(1)} %get-tuple-element.43.gy_ref), custom_call_target="tpu_custom_call" | custom-call | flops 603979776 | bytes 4194304 | tf_op jit(solution)/shard_map/wgrad_send/pallas_call | solution.py:343
  52.5 1.4 collective-permute-start.2
  53.9 1.7 collective-permute-start.3
  56.7 1.0 collective-permute-start.4
  57.8 2.2 %wgrad_keep.1 = bf16[768,768]{1,0:T(8,128)(2,1)S(1)} custom-call(s32[1]{0:T(128)} %bitcast.half_ref, bf16[512,1536]{1,0:T(8,128)(2,1)S(1)} %get-tuple-element.41.g_ref, bf16[512,768]{1,0:T(8,128)(2,1)S(1)} %get-tuple-element.42.n1_ref, bf16[512,768]{1,0:T(8,128)(2,1)S(1)} %get-tuple-element.43.gy_ref), custom_call_target="tpu_custom_call" | custom-call | flops 603979776 | bytes 4194304 | tf_op jit(solution)/shard_map/wgrad_keep/pallas_call | solution.py:343
  60.3 2.3 %fusion.7 = (bf16[1,192,768]{2,1,0:T(8,128)(2,1)S(1)}, bf16[1,192,768]{2,1,0:T(8,128)(2,1)S(1)}, bf16[1,192,768]{2,1,0:T(8,128)(2,1)S(1)}, f32[1,192,768]{2,1,0:T(8,128)}) fusion(bf16[1,4,192,768]{3,2,1,0:T(8,128)(2,1)} %bitcast.16, s32[]{:T(128)S(6)} %select_n.241, bf16[1,4,192,768]{3,2,1,0:T(8,128)(2,1)S(1)} %bitcast.165, s32[]{:T(128)S(6)} %select_n.249, ...), kind=kLoop, calls=%fused_computation.21 | loop fusion | flops 2211840 | bytes 3833872 | tf_op jit(solution)/shard_map/concatenate | solution.py:586
  62.6 1.4 collective-permute-start.5
  64.0 1.5 collective-permute-start.6
  65.6 1.7 collective-permute-start.7
  67.3 3.1 %collective-permute-done.5 = bf16[1,192,896]{2,1,0:T(8,128)(2,1)S(1)} collective-permute-done((bf16[1,192,896]{2,1,0:T(8,128)(2,1)S(1)}, bf16[1,192,896]{2,1,0:T(8,128)(2,1)S(1)}, u32[]{:S(2)}, u32[]{:S(2)}) %collective-permute-start.5) | collective-permute-done | bytes 344096 | tf_op jit(solution)/shard_map/ppermute | solution.py:52
  70.5 4.7 %collective-permute-done.7 = bf16[1,192,896]{2,1,0:T(8,128)(2,1)S(1)} collective-permute-done((bf16[1,192,896]{2,1,0:T(8,128)(2,1)S(1)}, bf16[1,192,896]{2,1,0:T(8,128)(2,1)S(1)}, u32[]{:S(2)}, u32[]{:S(2)}) %collective-permute-start.7) | collective-permute-done | bytes 344096 | tf_op jit(solution)/shard_map/ppermute | solution.py:52
  76.0 1.5 fusion.3
  77.5 0.8 copy-done.23
  78.4 2.8 %collective-permute-start.10 = (bf16[1,48,896]{2,1,0:T(8,128)(2,1)S(1)}, bf16[1,48,896]{2,1,0:T(8,128)(2,1)S(1)}, u32[]{:S(2)}, u32[]{:S(2)}) collective-permute-start(bf16[1,48,896]{2,1,0:T(8,128)(2,1)S(1)} %get-tuple-element.63), channel_id=1, source_target_pairs={{0,8},{2,34},{4,12},{6,38},{8,0},{10,42},{12,4},{14,46},{16,24},{1... | collective-permute-start | bytes 258056 | tf_op jit(solution)/shard_map/ppermute | solution.py:52
  81.7 2.1 %collective-permute-start.9 = (bf16[1,48,896]{2,1,0:T(8,128)(2,1)S(1)}, bf16[1,48,896]{2,1,0:T(8,128)(2,1)}, u32[]{:S(2)}, u32[]{:S(2)}) collective-permute-start(bf16[1,48,896]{2,1,0:T(8,128)(2,1)S(1)} %get-tuple-element.64), channel_id=1, source_target_pairs={{0,12},{2,50},{4,0},{6,54},{8,4},{10,58},{12,8},{14,62},{16,28},{1... | collective-permute-start | bytes 258056 | tf_op jit(solution)/shard_map/ppermute | solution.py:52
  83.8 2.0 collective-permute-done.8
  85.8 1.0 fusion.13
  86.9 3.5 %collective-permute-start.11 = (bf16[1,24,896]{2,1,0:T(8,128)(2,1)S(1)}, bf16[1,24,896]{2,1,0:T(8,128)(2,1)S(1)}, u32[]{:S(2)}, u32[]{:S(2)}) collective-permute-start(bf16[1,24,896]{2,1,0:T(8,128)(2,1)S(1)} %fusion.30), channel_id=1, source_target_pairs={{0,64},{2,66},{4,68},{6,70},{8,72},{10,74},{12,76},{14,78},{16,80}... | collective-permute-start | bytes 129032 | tf_op jit(solution)/shard_map/ppermute | solution.py:52
  90.4 1.4 collective-permute-done.11
  91.8 3.0 %collective-permute-start.12 = (bf16[1,24,896]{2,1,0:T(8,128)(2,1)S(1)}, bf16[1,24,896]{2,1,0:T(8,128)(2,1)S(1)}, u32[]{:S(2)}, u32[]{:S(2)}) collective-permute-start(bf16[1,24,896]{2,1,0:T(8,128)(2,1)S(1)} %fusion.25), channel_id=1, source_target_pairs={{0,64},{2,66},{4,68},{6,70},{8,72},{10,74},{12,76},{14,78},{16,80}... | collective-permute-start | bytes 129032 | tf_op jit(solution)/shard_map/ppermute | solution.py:52
  96.3 1.9 fusion.4
  98.3 1.0 collective-permute-start.24
  99.3 1.7 collective-permute-start.25
  101.0 0.8 collective-permute-start.26
  101.9 2.7 %collective-permute-start.13 = (bf16[1,48,896]{2,1,0:T(8,128)(2,1)S(1)}, bf16[1,48,896]{2,1,0:T(8,128)(2,1)S(1)}, u32[]{:S(2)}, u32[]{:S(2)}) collective-permute-start(bf16[1,48,896]{2,1,0:T(8,128)(2,1)S(1)} %bitcast.191), channel_id=1, source_target_pairs={{0,12},{2,50},{4,0},{6,54},{8,4},{10,58},{12,8},{14,62},{16,28},{1... | collective-permute-start | bytes 258056 | tf_op jit(solution)/shard_map/ppermute | solution.py:52
  104.6 1.5 collective-permute-done.13
  106.1 1.9 collective-permute-start.14
  108.1 3.8 %collective-permute-done.14 = bf16[1,48,896]{2,1,0:T(8,128)(2,1)S(1)} collective-permute-done((bf16[1,48,896]{2,1,0:T(8,128)(2,1)S(1)}, bf16[1,48,896]{2,1,0:T(8,128)(2,1)S(1)}, u32[]{:S(2)}, u32[]{:S(2)}) %collective-permute-start.14) | collective-permute-done | bytes 86048 | tf_op jit(solution)/shard_map/ppermute | solution.py:52
  111.9 1.0 collective-permute-start
  113.6 1.8 collective-permute-done.26
  115.4 1.4 fusion.1
  116.9 0.8 collective-permute-start.27
  117.7 2.3 %collective-permute-start.28 = (bf16[2,48,768]{2,1,0:T(8,128)(2,1)S(1)}, bf16[2,48,768]{2,1,0:T(8,128)(2,1)S(1)}, u32[]{:S(2)}, u32[]{:S(2)}) collective-permute-start(bf16[2,48,768]{2,1,0:T(8,128)(2,1)S(1)} %get-tuple-element.61), channel_id=1, source_target_pairs={{0,12},{2,50},{4,0},{6,54},{8,4},{10,58},{12,8},{14,62},{16,28},{1... | collective-permute-start | bytes 442376 | tf_op jit(solution)/shard_map/ppermute | solution.py:52
  121.2 3.8 %collective-permute-done.27 = bf16[2,48,768]{2,1,0:T(8,128)(2,1)S(1)} collective-permute-done((bf16[2,48,768]{2,1,0:T(8,128)(2,1)S(1)}, bf16[2,48,768]{2,1,0:T(8,128)(2,1)S(1)}, u32[]{:S(2)}, u32[]{:S(2)}) %collective-permute-start.27) | collective-permute-done | bytes 147488 | tf_op jit(solution)/shard_map/ppermute | solution.py:52
  125.0 1.6 collective-permute-done.29
  126.7 3.3 %collective-permute-start.30 = (bf16[2,24,768]{2,1,0:T(8,128)(2,1)S(1)}, bf16[2,24,768]{2,1,0:T(8,128)(2,1)S(1)}, u32[]{:S(2)}, u32[]{:S(2)}) collective-permute-start(bf16[2,24,768]{2,1,0:T(8,128)(2,1)S(1)} %fusion.26), channel_id=1, source_target_pairs={{0,64},{2,66},{4,68},{6,70},{8,72},{10,74},{12,76},{14,78},{16,80}... | collective-permute-start | bytes 221192 | tf_op jit(solution)/shard_map/ppermute | solution.py:52
  130.0 2.6 %collective-permute-done.30 = bf16[2,24,768]{2,1,0:T(8,128)(2,1)S(1)} collective-permute-done((bf16[2,24,768]{2,1,0:T(8,128)(2,1)S(1)}, bf16[2,24,768]{2,1,0:T(8,128)(2,1)S(1)}, u32[]{:S(2)}, u32[]{:S(2)}) %collective-permute-start.30) | collective-permute-done | bytes 73760 | tf_op jit(solution)/shard_map/ppermute | solution.py:52
  132.6 3.3 %collective-permute-start.31 = (bf16[2,24,768]{2,1,0:T(8,128)(2,1)S(1)}, bf16[2,24,768]{2,1,0:T(8,128)(2,1)S(1)}, u32[]{:S(2)}, u32[]{:S(2)}) collective-permute-start(bf16[2,24,768]{2,1,0:T(8,128)(2,1)S(1)} %fusion.17), channel_id=1, source_target_pairs={{0,64},{2,66},{4,68},{6,70},{8,72},{10,74},{12,76},{14,78},{16,80}... | collective-permute-start | bytes 221192 | tf_op jit(solution)/shard_map/ppermute | solution.py:52
  136.0 1.7 collective-permute-done.31
  137.8 2.4 %collective-permute-start.32 = (bf16[2,48,768]{2,1,0:T(8,128)(2,1)S(1)}, bf16[2,48,768]{2,1,0:T(8,128)(2,1)S(1)}, u32[]{:S(2)}, u32[]{:S(2)}) collective-permute-start(bf16[2,48,768]{2,1,0:T(8,128)(2,1)S(1)} %bitcast.184), channel_id=1, source_target_pairs={{0,12},{2,50},{4,0},{6,54},{8,4},{10,58},{12,8},{14,62},{16,28},{1... | collective-permute-start | bytes 442376 | tf_op jit(solution)/shard_map/ppermute | solution.py:52
  140.4 3.9 %collective-permute-start.17 = (bf16[1,192,896]{2,1,0:T(8,128)(2,1)S(1)}, bf16[1,192,896]{2,1,0:T(8,128)(2,1)S(1)}, u32[]{:S(2)}, u32[]{:S(2)}) collective-permute-start(bf16[1,192,896]{2,1,0:T(8,128)(2,1)S(1)} %bitcast.174), channel_id=1, source_target_pairs={{0,32},{2,10},{4,36},{6,14},{8,40},{10,2},{12,44},{14,6},{16,48},{... | collective-permute-start | bytes 1032200 | tf_op jit(solution)/shard_map/ppermute | solution.py:52
  144.4 5.5 %collective-permute-done.33 = bf16[2,48,768]{2,1,0:T(8,128)(2,1)S(1)} collective-permute-done((bf16[2,48,768]{2,1,0:T(8,128)(2,1)S(1)}, bf16[2,48,768]{2,1,0:T(8,128)(2,1)S(1)}, u32[]{:S(2)}, u32[]{:S(2)}) %collective-permute-start.33) | collective-permute-done | bytes 147488 | tf_op jit(solution)/shard_map/ppermute | solution.py:52
  149.9 5.6 %collective-permute-done.34 = bf16[2,48,768]{2,1,0:T(8,128)(2,1)S(1)} collective-permute-done((bf16[2,48,768]{2,1,0:T(8,128)(2,1)S(1)}, bf16[2,48,768]{2,1,0:T(8,128)(2,1)S(1)}, u32[]{:S(2)}, u32[]{:S(2)}) %collective-permute-start.34) | collective-permute-done | bytes 147488 | tf_op jit(solution)/shard_map/ppermute | solution.py:52
  155.5 2.1 %collective-permute-start.18 = (bf16[1,192,896]{2,1,0:T(8,128)(2,1)S(1)}, bf16[1,192,896]{2,1,0:T(8,128)(2,1)S(1)}, u32[]{:S(2)}, u32[]{:S(2)}) collective-permute-start(bf16[1,192,896]{2,1,0:T(8,128)(2,1)S(1)} %bitcast.175), channel_id=1, source_target_pairs={{0,48},{2,14},{4,52},{6,2},{8,56},{10,6},{12,60},{14,10},{16,0},{1... | collective-permute-start | bytes 1032200 | tf_op jit(solution)/shard_map/ppermute | solution.py:52
  157.8 12.4 %collective-permute-start.19 = (bf16[1,192,896]{2,1,0:T(8,128)(2,1)S(1)}, bf16[1,192,896]{2,1,0:T(8,128)(2,1)}, u32[]{:S(2)}, u32[]{:S(2)}) collective-permute-start(bf16[1,192,896]{2,1,0:T(8,128)(2,1)S(1)} %bitcast.176), channel_id=1, source_target_pairs={{0,2},{2,0},{4,6},{6,4},{8,10},{10,8},{12,14},{14,12},{16,18},{18,... | collective-permute-start | bytes 1032200 | tf_op jit(solution)/shard_map/ppermute | solution.py:52
  170.4 0.9 collective-permute-start.35
  171.3 2.1 %collective-permute-start.36 = (bf16[2,192,768]{2,1,0:T(8,128)(2,1)S(1)}, bf16[2,192,768]{2,1,0:T(8,128)(2,1)}, u32[]{:S(2)}, u32[]{:S(2)}) collective-permute-start(bf16[2,192,768]{2,1,0:T(8,128)(2,1)S(1)} %bitcast.167), channel_id=1, source_target_pairs={{0,32},{2,10},{4,36},{6,14},{8,40},{10,2},{12,44},{14,6},{16,48},{... | collective-permute-start | bytes 1769480 | tf_op jit(solution)/shard_map/ppermute | solution.py:52
  174.6 4.6 %collective-permute-start.21 = (bf16[1,192,896]{2,1,0:T(8,128)(2,1)}, bf16[1,192,896]{2,1,0:T(8,128)(2,1)}, u32[]{:S(2)}, u32[]{:S(2)}) collective-permute-start(bf16[1,192,896]{2,1,0:T(8,128)(2,1)} %copy-done.13), channel_id=1, source_target_pairs={{0,2},{2,0},{4,6},{6,4},{8,10},{10,8},{12,14},{14,12},{16,18},{18,... | collective-permute-start | bytes 1032200 | tf_op jit(solution)/shard_map/ppermute | solution.py:52
  179.4 2.6 %add_add_fusion = f32[512,768]{1,0:T(8,128)} fusion(f32[512,768]{1,0:T(8,128)S(1)} %copy-done.4, bf16[512,768]{1,0:T(8,128)(2,1)} %collective-permute-done.1, bf16[512,768]{1,0:T(8,128)(2,1)S(1)} %copy-done.6), kind=kLoop, calls=%fused_computation | loop fusion | flops 1572864 | bytes 4718592 | tf_op jit(solution)/shard_map/add | solution.py:595
  182.8 5.6 %collective-permute-start.39 = (bf16[2,192,768]{2,1,0:T(8,128)(2,1)}, bf16[2,192,768]{2,1,0:T(8,128)(2,1)S(1)}, u32[]{:S(2)}, u32[]{:S(2)}) collective-permute-start(bf16[2,192,768]{2,1,0:T(8,128)(2,1)} %collective-permute-done.35.refs_1_), channel_id=1, source_target_pairs={{0,2},{2,0},{4,6},{6,4},{8,10},{10,8},{12,14},{14,12},{16,18},{18,... | collective-permute-start | bytes 1769480 | tf_op jit(solution)/shard_map/ppermute | solution.py:52
  188.4 0.9 collective-permute-start.41
  189.2 1.2 add_convert_fusion
  190.5 4.3 %unpack_attn.1 = (f32[1152,768]{1,0:T(8,128)}, f32[384,768]{1,0:T(8,128)}, f32[64,128]{1,0:T(8,128)S(1)}) custom-call(s32[16]{0:T(128)S(1)} %stack.120.pos_ref, bf16[1,192,896]{2,1,0:T(8,128)(2,1)S(1)} %bitcast.177, bf16[1,192,896]{2,1,0:T(8,128)(2,1)} %collective-permute-done.16.refs_1_, bf16[1,192,896]{2,1,0:T(8,128)(2,1)S(1)} %copy-done.14, ...), custom_call_target="tpu_custom_call" | custom-call | bytes 8388608 | tf_op jit(solution)/shard_map/unpack_attn/pallas_call | solution.py:503
  196.7 6.0 %unpack_mlp.1 = (f32[1536,768]{1,0:T(8,128)}, f32[768,1536]{1,0:T(8,128)}) custom-call(s32[16]{0:T(128)S(1)} %stack.120.pos_ref, bf16[2,192,768]{2,1,0:T(8,128)(2,1)S(1)} %bitcast.170, bf16[2,192,768]{2,1,0:T(8,128)(2,1)} %collective-permute-done.35.refs_1_, bf16[2,192,768]{2,1,0:T(8,128)(2,1)} %collective-permute-done.36.refs_2_, ...), custom_call_target="tpu_custom_call" | custom-call | bytes 14680064 | tf_op jit(solution)/shard_map/unpack_mlp/pallas_call | solution.py:425
  (153 shorter events, 17.7 us)
Async XLA Ops:
  6.4 1.4 copy-start.2
  9.0 1.7 copy-start.17
  10.6 1.7 copy-start.18
  12.3 7.1 %copy-start.3 = (f32[512,768]{1,0:T(8,128)S(1)}, f32[512,768]{1,0:T(8,128)}, u32[]{:S(2)}) copy-start(f32[512,768]{1,0:T(8,128)} %cot_ref.1) | copy-start | bytes 4718596
  19.4 9.8 %copy-start.8 = (bf16[512,768]{1,0:T(8,128)(2,1)S(1)}, bf16[512,768]{1,0:T(8,128)(2,1)}, u32[]{:S(2)}) copy-start(bf16[512,768]{1,0:T(8,128)(2,1)} %x_ref.1) | copy-start | bytes 2359300
  19.4 9.8 %copy-start.19 = (bf16[6,64,768]{2,1,0:T(8,128)(2,1)S(1)}, bf16[6,64,768]{2,1,0:T(8,128)(2,1)}, u32[]{:S(2)}) copy-start(bf16[6,64,768]{2,1,0:T(8,128)(2,1)} %param.24) | copy-start | bytes 1769476
  19.5 9.8 %copy-start.20 = (f32[1,128]{1,0:T(1,128)S(1)}, f32[1,128]{1,0:T(1,128)}, u32[]{:S(2)}) copy-start(f32[1,128]{1,0:T(1,128)} %constant.229.clone.freq_ref) | copy-start | bytes 1540
  48.9 3.6 %copy-start.5 = (bf16[512,768]{1,0:T(8,128)(2,1)}, bf16[512,768]{1,0:T(8,128)(2,1)S(1)}, u32[]{:S(2)}) copy-start(bf16[512,768]{1,0:T(8,128)(2,1)S(1)} %get-tuple-element.40) | copy-start | bytes 2359300
  48.9 3.6 %copy-start.10 = (bf16[512,768]{1,0:T(8,128)(2,1)}, bf16[512,768]{1,0:T(8,128)(2,1)S(1)}, u32[]{:S(2)}) copy-start(bf16[512,768]{1,0:T(8,128)(2,1)S(1)} %get-tuple-element.39) | copy-start | bytes 2359300
  52.5 7.8 %collective-permute-start.2 = (bf16[768,768]{1,0:T(8,128)(2,1)}, bf16[768,768]{1,0:T(8,128)(2,1)}, u32[]{:S(2)}, u32[]{:S(2)}) collective-permute-start(bf16[768,768]{1,0:T(8,128)(2,1)} %wgrad_send.1), channel_id=1, source_target_pairs={{0,2},{2,0},{4,6},{6,4},{8,10},{10,8},{12,14},{14,12},{16,18},{18,... | collective-permute-start | bytes 3538952 | tf_op jit(solution)/shard_map/ppermute | solution.py:52
  53.9 2.8 %collective-permute-start.3 = (f32[24,128]{1,0:T(8,128)S(1)}, f32[24,128]{1,0:T(8,128)S(1)}, u32[]{:S(2)}, u32[]{:S(2)}) collective-permute-start(f32[24,128]{1,0:T(8,128)S(1)} %slice.28), channel_id=1, source_target_pairs={{0,1},{1,0},{2,3},{3,2},{4,5},{5,4},{6,7},{7,6},{8,9},{9,8},{10,11... | collective-permute-start | bytes 36872 | tf_op jit(solution)/shard_map/ppermute | solution.py:576
  55.7 40.7 %collective-permute-start.23 = (bf16[2,768,768]{2,1,0:T(8,128)(2,1)}, bf16[2,768,768]{2,1,0:T(8,128)(2,1)}, u32[]{:S(2)}, u32[]{:S(2)}) collective-permute-start(bf16[2,768,768]{2,1,0:T(8,128)(2,1)} %get-tuple-element.49), channel_id=1, source_target_pairs={{0,2},{2,0},{4,6},{6,4},{8,10},{10,8},{12,14},{14,12},{16,18},{18,... | collective-permute-start | bytes 7077896 | tf_op jit(solution)/shard_map/ppermute | solution.py:52
  56.7 3.5 %collective-permute-start.4 = (f32[64,128]{1,0:T(8,128)S(1)}, f32[64,128]{1,0:T(8,128)S(1)}, u32[]{:S(2)}, u32[]{:S(2)}) collective-permute-start(f32[64,128]{1,0:T(8,128)S(1)} %pad_maximum_fusion.5), channel_id=1, source_target_pairs={{0,2},{2,0},{4,6},{6,4},{8,10},{10,8},{12,14},{14,12},{16,18},{18,... | collective-permute-start | bytes 98312 | tf_op jit(solution)/shard_map/ppermute | solution.py:52
  62.6 7.7 %collective-permute-start.5 = (bf16[1,192,896]{2,1,0:T(8,128)(2,1)S(1)}, bf16[1,192,896]{2,1,0:T(8,128)(2,1)S(1)}, u32[]{:S(2)}, u32[]{:S(2)}) collective-permute-start(bf16[1,192,896]{2,1,0:T(8,128)(2,1)S(1)} %pad_maximum_fusion), channel_id=1, source_target_pairs={{0,16},{2,6},{4,20},{6,10},{8,24},{10,14},{12,28},{14,2},{16,32},{... | collective-permute-start | bytes 1032200 | tf_op jit(solution)/shard_map/ppermute | solution.py:52
  64.0 6.5 %collective-permute-start.6 = (bf16[1,192,896]{2,1,0:T(8,128)(2,1)S(1)}, bf16[1,192,896]{2,1,0:T(8,128)(2,1)S(1)}, u32[]{:S(2)}, u32[]{:S(2)}) collective-permute-start(bf16[1,192,896]{2,1,0:T(8,128)(2,1)S(1)} %pad_maximum_fusion.1), channel_id=1, source_target_pairs={{0,48},{2,14},{4,52},{6,2},{8,56},{10,6},{12,60},{14,10},{16,0},{1... | collective-permute-start | bytes 1032200 | tf_op jit(solution)/shard_map/ppermute | solution.py:52
  65.6 9.6 %collective-permute-start.7 = (bf16[1,192,896]{2,1,0:T(8,128)(2,1)S(1)}, bf16[1,192,896]{2,1,0:T(8,128)(2,1)S(1)}, u32[]{:S(2)}, u32[]{:S(2)}) collective-permute-start(bf16[1,192,896]{2,1,0:T(8,128)(2,1)S(1)} %pad_maximum_fusion.2), channel_id=1, source_target_pairs={{0,32},{2,10},{4,36},{6,14},{8,40},{10,2},{12,44},{14,6},{16,48},{... | collective-permute-start | bytes 1032200 | tf_op jit(solution)/shard_map/ppermute | solution.py:52
  70.5 4.7 %copy-start.26 = (bf16[1,192,896]{2,1,0:T(8,128)(2,1)}, bf16[1,192,896]{2,1,0:T(8,128)(2,1)S(1)}, u32[]{:S(2)}) copy-start(bf16[1,192,896]{2,1,0:T(8,128)(2,1)S(1)} %collective-permute-done.6) | copy-start | bytes 1032196
  76.0 18.9 %copy-start.6 = (bf16[512,768]{1,0:T(8,128)(2,1)S(1)}, bf16[512,768]{1,0:T(8,128)(2,1)}, u32[]{:S(2)}) copy-start(bf16[512,768]{1,0:T(8,128)(2,1)} %copy-done.5) | copy-start | bytes 2359300
  76.0 20.4 %copy-start.1 = (bf16[2,768,768]{2,1,0:T(8,128)(2,1)S(1)}, bf16[2,768,768]{2,1,0:T(8,128)(2,1)}, u32[]{:S(2)}) copy-start(bf16[2,768,768]{2,1,0:T(8,128)(2,1)} %copy-done) | copy-start | bytes 7077892
  78.4 5.4 %collective-permute-start.10 = (bf16[1,48,896]{2,1,0:T(8,128)(2,1)S(1)}, bf16[1,48,896]{2,1,0:T(8,128)(2,1)S(1)}, u32[]{:S(2)}, u32[]{:S(2)}) collective-permute-start(bf16[1,48,896]{2,1,0:T(8,128)(2,1)S(1)} %get-tuple-element.63), channel_id=1, source_target_pairs={{0,8},{2,34},{4,12},{6,38},{8,0},{10,42},{12,4},{14,46},{16,24},{1... | collective-permute-start | bytes 258056 | tf_op jit(solution)/shard_map/ppermute | solution.py:52
  81.2 4.7 %collective-permute-start.8 = (bf16[1,48,896]{2,1,0:T(8,128)(2,1)S(1)}, bf16[1,48,896]{2,1,0:T(8,128)(2,1)}, u32[]{:S(2)}, u32[]{:S(2)}) collective-permute-start(bf16[1,48,896]{2,1,0:T(8,128)(2,1)S(1)} %get-tuple-element.62), channel_id=1, source_target_pairs={{0,4},{2,18},{4,8},{6,22},{8,12},{10,26},{12,0},{14,30},{16,20},{1... | collective-permute-start | bytes 258056 | tf_op jit(solution)/shard_map/ppermute | solution.py:52
  81.7 4.1 %collective-permute-start.9 = (bf16[1,48,896]{2,1,0:T(8,128)(2,1)S(1)}, bf16[1,48,896]{2,1,0:T(8,128)(2,1)}, u32[]{:S(2)}, u32[]{:S(2)}) collective-permute-start(bf16[1,48,896]{2,1,0:T(8,128)(2,1)S(1)} %get-tuple-element.64), channel_id=1, source_target_pairs={{0,12},{2,50},{4,0},{6,54},{8,4},{10,58},{12,8},{14,62},{16,28},{1... | collective-permute-start | bytes 258056 | tf_op jit(solution)/shard_map/ppermute | solution.py:52
  86.9 4.9 %collective-permute-start.11 = (bf16[1,24,896]{2,1,0:T(8,128)(2,1)S(1)}, bf16[1,24,896]{2,1,0:T(8,128)(2,1)S(1)}, u32[]{:S(2)}, u32[]{:S(2)}) collective-permute-start(bf16[1,24,896]{2,1,0:T(8,128)(2,1)S(1)} %fusion.30), channel_id=1, source_target_pairs={{0,64},{2,66},{4,68},{6,70},{8,72},{10,74},{12,76},{14,78},{16,80}... | collective-permute-start | bytes 129032 | tf_op jit(solution)/shard_map/ppermute | solution.py:52
  91.8 4.5 %collective-permute-start.12 = (bf16[1,24,896]{2,1,0:T(8,128)(2,1)S(1)}, bf16[1,24,896]{2,1,0:T(8,128)(2,1)S(1)}, u32[]{:S(2)}, u32[]{:S(2)}) collective-permute-start(bf16[1,24,896]{2,1,0:T(8,128)(2,1)S(1)} %fusion.25), channel_id=1, source_target_pairs={{0,64},{2,66},{4,68},{6,70},{8,72},{10,74},{12,76},{14,78},{16,80}... | collective-permute-start | bytes 129032 | tf_op jit(solution)/shard_map/ppermute | solution.py:52
  94.9 62.9 %collective-permute-start.1 = (bf16[512,768]{1,0:T(8,128)(2,1)S(1)}, bf16[512,768]{1,0:T(8,128)(2,1)}, u32[]{:S(2)}, u32[]{:S(2)}) collective-permute-start(bf16[512,768]{1,0:T(8,128)(2,1)S(1)} %copy-done.6), channel_id=1, source_target_pairs={{0,1},{1,0},{2,3},{3,2},{4,5},{5,4},{6,7},{7,6},{8,9},{9,8},{10,11... | collective-permute-start | bytes 2359304 | tf_op jit(solution)/shard_map/ppermute | solution.py:591
  96.3 15.6 %copy-start.11 = (bf16[512,768]{1,0:T(8,128)(2,1)S(1)}, bf16[512,768]{1,0:T(8,128)(2,1)}, u32[]{:S(2)}) copy-start(bf16[512,768]{1,0:T(8,128)(2,1)} %copy-done.10) | copy-start | bytes 2359300
  98.3 14.6 %collective-permute-start.24 = (bf16[2,192,768]{2,1,0:T(8,128)(2,1)S(1)}, bf16[2,192,768]{2,1,0:T(8,128)(2,1)S(1)}, u32[]{:S(2)}, u32[]{:S(2)}) collective-permute-start(bf16[2,192,768]{2,1,0:T(8,128)(2,1)S(1)} %get-tuple-element.52), channel_id=1, source_target_pairs={{0,16},{2,6},{4,20},{6,10},{8,24},{10,14},{12,28},{14,2},{16,32},{... | collective-permute-start | bytes 1769480 | tf_op jit(solution)/shard_map/ppermute | solution.py:52
  99.3 14.3 %collective-permute-start.25 = (bf16[2,192,768]{2,1,0:T(8,128)(2,1)S(1)}, bf16[2,192,768]{2,1,0:T(8,128)(2,1)S(1)}, u32[]{:S(2)}, u32[]{:S(2)}) collective-permute-start(bf16[2,192,768]{2,1,0:T(8,128)(2,1)S(1)} %get-tuple-element.53), channel_id=1, source_target_pairs={{0,48},{2,14},{4,52},{6,2},{8,56},{10,6},{12,60},{14,10},{16,0},{1... | collective-permute-start | bytes 1769480 | tf_op jit(solution)/shard_map/ppermute | solution.py:52
  101.0 14.4 %collective-permute-start.26 = (bf16[2,192,768]{2,1,0:T(8,128)(2,1)S(1)}, bf16[2,192,768]{2,1,0:T(8,128)(2,1)S(1)}, u32[]{:S(2)}, u32[]{:S(2)}) collective-permute-start(bf16[2,192,768]{2,1,0:T(8,128)(2,1)S(1)} %get-tuple-element.54), channel_id=1, source_target_pairs={{0,32},{2,10},{4,36},{6,14},{8,40},{10,2},{12,44},{14,6},{16,48},{... | collective-permute-start | bytes 1769480 | tf_op jit(solution)/shard_map/ppermute | solution.py:52
  101.9 4.3 %collective-permute-start.13 = (bf16[1,48,896]{2,1,0:T(8,128)(2,1)S(1)}, bf16[1,48,896]{2,1,0:T(8,128)(2,1)S(1)}, u32[]{:S(2)}, u32[]{:S(2)}) collective-permute-start(bf16[1,48,896]{2,1,0:T(8,128)(2,1)S(1)} %bitcast.191), channel_id=1, source_target_pairs={{0,12},{2,50},{4,0},{6,54},{8,4},{10,58},{12,8},{14,62},{16,28},{1... | collective-permute-start | bytes 258056 | tf_op jit(solution)/shard_map/ppermute | solution.py:52
  106.1 5.8 %collective-permute-start.14 = (bf16[1,48,896]{2,1,0:T(8,128)(2,1)S(1)}, bf16[1,48,896]{2,1,0:T(8,128)(2,1)S(1)}, u32[]{:S(2)}, u32[]{:S(2)}) collective-permute-start(bf16[1,48,896]{2,1,0:T(8,128)(2,1)S(1)} %bitcast.193), channel_id=1, source_target_pairs={{0,8},{2,34},{4,12},{6,38},{8,0},{10,42},{12,4},{14,46},{16,24},{1... | collective-permute-start | bytes 258056 | tf_op jit(solution)/shard_map/ppermute | solution.py:52
  111.9 58.4 %collective-permute-start = (bf16[512,768]{1,0:T(8,128)(2,1)S(1)}, bf16[512,768]{1,0:T(8,128)(2,1)S(1)}, u32[]{:S(2)}, u32[]{:S(2)}) collective-permute-start(bf16[512,768]{1,0:T(8,128)(2,1)S(1)} %copy-done.11), channel_id=1, source_target_pairs={{0,1},{1,0},{2,3},{3,2},{4,5},{5,4},{6,7},{7,6},{8,9},{9,8},{10,11... | collective-permute-start | bytes 2359304 | tf_op jit(solution)/shard_map/ppermute | solution.py:590
  112.9 7.5 %collective-permute-start.15 = (bf16[1,48,896]{2,1,0:T(8,128)(2,1)S(1)}, bf16[1,48,896]{2,1,0:T(8,128)(2,1)S(1)}, u32[]{:S(2)}, u32[]{:S(2)}) collective-permute-start(bf16[1,48,896]{2,1,0:T(8,128)(2,1)S(1)} %bitcast.194), channel_id=1, source_target_pairs={{0,4},{2,18},{4,8},{6,22},{8,12},{10,26},{12,0},{14,30},{16,20},{1... | collective-permute-start | bytes 258056 | tf_op jit(solution)/shard_map/ppermute | solution.py:52
  116.9 8.1 %collective-permute-start.27 = (bf16[2,48,768]{2,1,0:T(8,128)(2,1)S(1)}, bf16[2,48,768]{2,1,0:T(8,128)(2,1)S(1)}, u32[]{:S(2)}, u32[]{:S(2)}) collective-permute-start(bf16[2,48,768]{2,1,0:T(8,128)(2,1)S(1)} %get-tuple-element.59), channel_id=1, source_target_pairs={{0,4},{2,18},{4,8},{6,22},{8,12},{10,26},{12,0},{14,30},{16,20},{1... | collective-permute-start | bytes 442376 | tf_op jit(solution)/shard_map/ppermute | solution.py:52
  117.7 7.3 %collective-permute-start.28 = (bf16[2,48,768]{2,1,0:T(8,128)(2,1)S(1)}, bf16[2,48,768]{2,1,0:T(8,128)(2,1)S(1)}, u32[]{:S(2)}, u32[]{:S(2)}) collective-permute-start(bf16[2,48,768]{2,1,0:T(8,128)(2,1)S(1)} %get-tuple-element.61), channel_id=1, source_target_pairs={{0,12},{2,50},{4,0},{6,54},{8,4},{10,58},{12,8},{14,62},{16,28},{1... | collective-permute-start | bytes 442376 | tf_op jit(solution)/shard_map/ppermute | solution.py:52
  120.4 6.2 %collective-permute-start.29 = (bf16[2,48,768]{2,1,0:T(8,128)(2,1)S(1)}, bf16[2,48,768]{2,1,0:T(8,128)(2,1)S(1)}, u32[]{:S(2)}, u32[]{:S(2)}) collective-permute-start(bf16[2,48,768]{2,1,0:T(8,128)(2,1)S(1)} %get-tuple-element.60), channel_id=1, source_target_pairs={{0,8},{2,34},{4,12},{6,38},{8,0},{10,42},{12,4},{14,46},{16,24},{1... | collective-permute-start | bytes 442376 | tf_op jit(solution)/shard_map/ppermute | solution.py:52
  126.7 5.9 %collective-permute-start.30 = (bf16[2,24,768]{2,1,0:T(8,128)(2,1)S(1)}, bf16[2,24,768]{2,1,0:T(8,128)(2,1)S(1)}, u32[]{:S(2)}, u32[]{:S(2)}) collective-permute-start(bf16[2,24,768]{2,1,0:T(8,128)(2,1)S(1)} %fusion.26), channel_id=1, source_target_pairs={{0,64},{2,66},{4,68},{6,70},{8,72},{10,74},{12,76},{14,78},{16,80}... | collective-permute-start | bytes 221192 | tf_op jit(solution)/shard_map/ppermute | solution.py:52
  132.6 5.1 %collective-permute-start.31 = (bf16[2,24,768]{2,1,0:T(8,128)(2,1)S(1)}, bf16[2,24,768]{2,1,0:T(8,128)(2,1)S(1)}, u32[]{:S(2)}, u32[]{:S(2)}) collective-permute-start(bf16[2,24,768]{2,1,0:T(8,128)(2,1)S(1)} %fusion.17), channel_id=1, source_target_pairs={{0,64},{2,66},{4,68},{6,70},{8,72},{10,74},{12,76},{14,78},{16,80}... | collective-permute-start | bytes 221192 | tf_op jit(solution)/shard_map/ppermute | solution.py:52
  137.8 6.5 %collective-permute-start.32 = (bf16[2,48,768]{2,1,0:T(8,128)(2,1)S(1)}, bf16[2,48,768]{2,1,0:T(8,128)(2,1)S(1)}, u32[]{:S(2)}, u32[]{:S(2)}) collective-permute-start(bf16[2,48,768]{2,1,0:T(8,128)(2,1)S(1)} %bitcast.184), channel_id=1, source_target_pairs={{0,12},{2,50},{4,0},{6,54},{8,4},{10,58},{12,8},{14,62},{16,28},{1... | collective-permute-start | bytes 442376 | tf_op jit(solution)/shard_map/ppermute | solution.py:52
  140.2 30.0 %collective-permute-start.16 = (bf16[1,192,896]{2,1,0:T(8,128)(2,1)S(1)}, bf16[1,192,896]{2,1,0:T(8,128)(2,1)}, u32[]{:S(2)}, u32[]{:S(2)}) collective-permute-start(bf16[1,192,896]{2,1,0:T(8,128)(2,1)S(1)} %bitcast.173), channel_id=1, source_target_pairs={{0,16},{2,6},{4,20},{6,10},{8,24},{10,14},{12,28},{14,2},{16,32},{... | collective-permute-start | bytes 1032200 | tf_op jit(solution)/shard_map/ppermute | solution.py:52
  140.4 30.9 %collective-permute-start.17 = (bf16[1,192,896]{2,1,0:T(8,128)(2,1)S(1)}, bf16[1,192,896]{2,1,0:T(8,128)(2,1)S(1)}, u32[]{:S(2)}, u32[]{:S(2)}) collective-permute-start(bf16[1,192,896]{2,1,0:T(8,128)(2,1)S(1)} %bitcast.174), channel_id=1, source_target_pairs={{0,32},{2,10},{4,36},{6,14},{8,40},{10,2},{12,44},{14,6},{16,48},{... | collective-permute-start | bytes 1032200 | tf_op jit(solution)/shard_map/ppermute | solution.py:52
  144.3 5.6 %collective-permute-start.33 = (bf16[2,48,768]{2,1,0:T(8,128)(2,1)S(1)}, bf16[2,48,768]{2,1,0:T(8,128)(2,1)S(1)}, u32[]{:S(2)}, u32[]{:S(2)}) collective-permute-start(bf16[2,48,768]{2,1,0:T(8,128)(2,1)S(1)} %bitcast.186), channel_id=1, source_target_pairs={{0,8},{2,34},{4,12},{6,38},{8,0},{10,42},{12,4},{14,46},{16,24},{1... | collective-permute-start | bytes 442376 | tf_op jit(solution)/shard_map/ppermute | solution.py:52
  149.9 5.6 %collective-permute-start.34 = (bf16[2,48,768]{2,1,0:T(8,128)(2,1)S(1)}, bf16[2,48,768]{2,1,0:T(8,128)(2,1)S(1)}, u32[]{:S(2)}, u32[]{:S(2)}) collective-permute-start(bf16[2,48,768]{2,1,0:T(8,128)(2,1)S(1)} %bitcast.187), channel_id=1, source_target_pairs={{0,4},{2,18},{4,8},{6,22},{8,12},{10,26},{12,0},{14,30},{16,20},{1... | collective-permute-start | bytes 442376 | tf_op jit(solution)/shard_map/ppermute | solution.py:52
  155.5 17.8 %collective-permute-start.18 = (bf16[1,192,896]{2,1,0:T(8,128)(2,1)S(1)}, bf16[1,192,896]{2,1,0:T(8,128)(2,1)S(1)}, u32[]{:S(2)}, u32[]{:S(2)}) collective-permute-start(bf16[1,192,896]{2,1,0:T(8,128)(2,1)S(1)} %bitcast.175), channel_id=1, source_target_pairs={{0,48},{2,14},{4,52},{6,2},{8,56},{10,6},{12,60},{14,10},{16,0},{1... | collective-permute-start | bytes 1032200 | tf_op jit(solution)/shard_map/ppermute | solution.py:52
  157.7 21.7 %copy-start.4 = (f32[512,768]{1,0:T(8,128)S(1)}, f32[512,768]{1,0:T(8,128)}, u32[]{:S(2)}) copy-start(f32[512,768]{1,0:T(8,128)} %cot_ref.1) | copy-start | bytes 4718596
  157.8 16.8 %collective-permute-start.19 = (bf16[1,192,896]{2,1,0:T(8,128)(2,1)S(1)}, bf16[1,192,896]{2,1,0:T(8,128)(2,1)}, u32[]{:S(2)}, u32[]{:S(2)}) collective-permute-start(bf16[1,192,896]{2,1,0:T(8,128)(2,1)S(1)} %bitcast.176), channel_id=1, source_target_pairs={{0,2},{2,0},{4,6},{6,4},{8,10},{10,8},{12,14},{14,12},{16,18},{18,... | collective-permute-start | bytes 1032200 | tf_op jit(solution)/shard_map/ppermute | solution.py:52
  170.1 9.2 %collective-permute-start.20 = (bf16[1,192,896]{2,1,0:T(8,128)(2,1)}, bf16[1,192,896]{2,1,0:T(8,128)(2,1)}, u32[]{:S(2)}, u32[]{:S(2)}) collective-permute-start(bf16[1,192,896]{2,1,0:T(8,128)(2,1)} %collective-permute-done.16.refs_1_), channel_id=1, source_target_pairs={{0,2},{2,0},{4,6},{6,4},{8,10},{10,8},{12,14},{14,12},{16,18},{18,... | collective-permute-start | bytes 1032200 | tf_op jit(solution)/shard_map/ppermute | solution.py:52
  170.3 3.0 %copy-start.24 = (bf16[512,768]{1,0:T(8,128)(2,1)}, bf16[512,768]{1,0:T(8,128)(2,1)S(1)}, u32[]{:S(2)}) copy-start(bf16[512,768]{1,0:T(8,128)(2,1)S(1)} %collective-permute-done) | copy-start | bytes 2359300
  170.4 12.4 %collective-permute-start.35 = (bf16[2,192,768]{2,1,0:T(8,128)(2,1)S(1)}, bf16[2,192,768]{2,1,0:T(8,128)(2,1)}, u32[]{:S(2)}, u32[]{:S(2)}) collective-permute-start(bf16[2,192,768]{2,1,0:T(8,128)(2,1)S(1)} %bitcast.166), channel_id=1, source_target_pairs={{0,16},{2,6},{4,20},{6,10},{8,24},{10,14},{12,28},{14,2},{16,32},{... | collective-permute-start | bytes 1769480 | tf_op jit(solution)/shard_map/ppermute | solution.py:52
  171.3 2.1 %copy-start.13 = (bf16[1,192,896]{2,1,0:T(8,128)(2,1)}, bf16[1,192,896]{2,1,0:T(8,128)(2,1)S(1)}, u32[]{:S(2)}) copy-start(bf16[1,192,896]{2,1,0:T(8,128)(2,1)S(1)} %collective-permute-done.17.refs_2_) | copy-start | bytes 1032196
  171.3 17.1 %collective-permute-start.36 = (bf16[2,192,768]{2,1,0:T(8,128)(2,1)S(1)}, bf16[2,192,768]{2,1,0:T(8,128)(2,1)}, u32[]{:S(2)}, u32[]{:S(2)}) collective-permute-start(bf16[2,192,768]{2,1,0:T(8,128)(2,1)S(1)} %bitcast.167), channel_id=1, source_target_pairs={{0,32},{2,10},{4,36},{6,14},{8,40},{10,2},{12,44},{14,6},{16,48},{... | collective-permute-start | bytes 1769480 | tf_op jit(solution)/shard_map/ppermute | solution.py:52
  174.1 14.3 %collective-permute-start.37 = (bf16[2,192,768]{2,1,0:T(8,128)(2,1)S(1)}, bf16[2,192,768]{2,1,0:T(8,128)(2,1)}, u32[]{:S(2)}, u32[]{:S(2)}) collective-permute-start(bf16[2,192,768]{2,1,0:T(8,128)(2,1)S(1)} %bitcast.168), channel_id=1, source_target_pairs={{0,48},{2,14},{4,52},{6,2},{8,56},{10,6},{12,60},{14,10},{16,0},{1... | collective-permute-start | bytes 1769480 | tf_op jit(solution)/shard_map/ppermute | solution.py:52
  174.6 7.5 %collective-permute-start.21 = (bf16[1,192,896]{2,1,0:T(8,128)(2,1)}, bf16[1,192,896]{2,1,0:T(8,128)(2,1)}, u32[]{:S(2)}, u32[]{:S(2)}) collective-permute-start(bf16[1,192,896]{2,1,0:T(8,128)(2,1)} %copy-done.13), channel_id=1, source_target_pairs={{0,2},{2,0},{4,6},{6,4},{8,10},{10,8},{12,14},{14,12},{16,18},{18,... | collective-permute-start | bytes 1032200 | tf_op jit(solution)/shard_map/ppermute | solution.py:52
  179.3 10.0 %copy-start.9 = (bf16[512,768]{1,0:T(8,128)(2,1)S(1)}, bf16[512,768]{1,0:T(8,128)(2,1)}, u32[]{:S(2)}) copy-start(bf16[512,768]{1,0:T(8,128)(2,1)} %x_ref.1) | copy-start | bytes 2359300
  179.3 10.0 %copy-start.12 = (bf16[512,768]{1,0:T(8,128)(2,1)S(1)}, bf16[512,768]{1,0:T(8,128)(2,1)}, u32[]{:S(2)}) copy-start(bf16[512,768]{1,0:T(8,128)(2,1)} %copy-done.10) | copy-start | bytes 2359300
  179.3 9.9 %copy-start.25 = (bf16[512,768]{1,0:T(8,128)(2,1)S(1)}, bf16[512,768]{1,0:T(8,128)(2,1)}, u32[]{:S(2)}) copy-start(bf16[512,768]{1,0:T(8,128)(2,1)} %copy-done.24) | copy-start | bytes 2359300
  179.3 11.2 %collective-permute-start.22 = (bf16[1,192,896]{2,1,0:T(8,128)(2,1)}, bf16[1,192,896]{2,1,0:T(8,128)(2,1)S(1)}, u32[]{:S(2)}, u32[]{:S(2)}) collective-permute-start(bf16[1,192,896]{2,1,0:T(8,128)(2,1)} %copy-done.15), channel_id=1, source_target_pairs={{0,2},{2,0},{4,6},{6,4},{8,10},{10,8},{12,14},{14,12},{16,18},{18,... | collective-permute-start | bytes 1032200 | tf_op jit(solution)/shard_map/ppermute | solution.py:52
  182.0 8.4 %copy-start.14 = (bf16[1,192,896]{2,1,0:T(8,128)(2,1)S(1)}, bf16[1,192,896]{2,1,0:T(8,128)(2,1)}, u32[]{:S(2)}) copy-start(bf16[1,192,896]{2,1,0:T(8,128)(2,1)} %copy-done.13) | copy-start | bytes 1032196
  182.0 8.4 %copy-start.16 = (bf16[1,192,896]{2,1,0:T(8,128)(2,1)S(1)}, bf16[1,192,896]{2,1,0:T(8,128)(2,1)}, u32[]{:S(2)}) copy-start(bf16[1,192,896]{2,1,0:T(8,128)(2,1)} %copy-done.15) | copy-start | bytes 1032196
  182.0 14.7 %collective-permute-start.38 = (bf16[2,192,768]{2,1,0:T(8,128)(2,1)S(1)}, bf16[2,192,768]{2,1,0:T(8,128)(2,1)S(1)}, u32[]{:S(2)}, u32[]{:S(2)}) collective-permute-start(bf16[2,192,768]{2,1,0:T(8,128)(2,1)S(1)} %bitcast.169), channel_id=1, source_target_pairs={{0,2},{2,0},{4,6},{6,4},{8,10},{10,8},{12,14},{14,12},{16,18},{18,... | collective-permute-start | bytes 1769480 | tf_op jit(solution)/shard_map/ppermute | solution.py:52
  182.8 13.9 %collective-permute-start.39 = (bf16[2,192,768]{2,1,0:T(8,128)(2,1)}, bf16[2,192,768]{2,1,0:T(8,128)(2,1)S(1)}, u32[]{:S(2)}, u32[]{:S(2)}) collective-permute-start(bf16[2,192,768]{2,1,0:T(8,128)(2,1)} %collective-permute-done.35.refs_1_), channel_id=1, source_target_pairs={{0,2},{2,0},{4,6},{6,4},{8,10},{10,8},{12,14},{14,12},{16,18},{18,... | collective-permute-start | bytes 1769480 | tf_op jit(solution)/shard_map/ppermute | solution.py:52
  188.4 8.4 %collective-permute-start.40 = (bf16[2,192,768]{2,1,0:T(8,128)(2,1)}, bf16[2,192,768]{2,1,0:T(8,128)(2,1)S(1)}, u32[]{:S(2)}, u32[]{:S(2)}) collective-permute-start(bf16[2,192,768]{2,1,0:T(8,128)(2,1)} %collective-permute-done.36.refs_2_), channel_id=1, source_target_pairs={{0,2},{2,0},{4,6},{6,4},{8,10},{10,8},{12,14},{14,12},{16,18},{18,... | collective-permute-start | bytes 1769480 | tf_op jit(solution)/shard_map/ppermute | solution.py:52
  188.4 8.4 %collective-permute-start.41 = (bf16[2,192,768]{2,1,0:T(8,128)(2,1)}, bf16[2,192,768]{2,1,0:T(8,128)(2,1)}, u32[]{:S(2)}, u32[]{:S(2)}) collective-permute-start(bf16[2,192,768]{2,1,0:T(8,128)(2,1)} %collective-permute-done.37.refs_3_), channel_id=1, source_target_pairs={{0,2},{2,0},{4,6},{6,4},{8,10},{10,8},{12,14},{14,12},{16,18},{18,... | collective-permute-start | bytes 1769480 | tf_op jit(solution)/shard_map/ppermute | solution.py:52
  196.1 6.6 %copy-start.28 = (f32[768]{0:T(1024)}, f32[768]{0:T(1024)S(1)}, u32[]{:S(2)}) copy-start(f32[768]{0:T(1024)S(1)} %get-tuple-element.104) | copy-start | bytes 9220
  (7 other events, 7.1 us)

commit v2 on v1

--- a/solution.py
+++ b/solution.py
@@ -73,17 +73,17 @@
 
 def mlp_kernel(first, half_ref, *refs):
     if first:
-        (x_ref, cot_ref, vec_ref, bfc_ref, wfc_ref, wproj_ref,
+        (x_ref, cot_ref, g_ref, b_ref, bfc_ref, wfc_ref, wproj_ref,
          gw_ref, gm_ref, mo_ref, gb_ref, normed, gy) = refs
     else:
-        (x_ref, cot_ref, vec_ref, bfc_ref, wfc_ref, wproj_ref, gm_in, mo_in,
+        (x_ref, cot_ref, g_ref, b_ref, bfc_ref, wfc_ref, wproj_ref, gm_in, mo_in,
          gw_ref, gm_ref, mo_ref, gb_ref, normed, gy) = refs
     i = pl.program_id(0)
 
     @pl.when(i == 0)
     def _():
         n, _unused = norm_parts(x_ref[...])
-        normed[...] = (n * vec_ref[2:3, :] + vec_ref[3:4, :]).astype(BF)
+        normed[...] = (n * as_row(g_ref) + as_row(b_ref)).astype(BF)
         gy[...] = cot_ref[...].astype(BF)
         if first:
             gm_ref[...] = jnp.zeros_like(gm_ref)
@@ -94,7 +94,7 @@
 
     wfc = wfc_ref[...]
     wproj = wproj_ref[...]
-    hidden = dot(normed[...], wfc) + bfc_ref[...]
+    hidden = dot(normed[...], wfc) + bfc_ref[:, pl.ds(pl.multiple_of((half_ref[0] * 3 + i) * 256, 256), 256)]
     cdf = 0.5 * (1.0 + lax.erf(hidden * np.float32(np.sqrt(0.5))))
     pdf = jnp.exp(-0.5 * hidden * hidden) * np.float32(1.0 / np.sqrt(2.0 * np.pi))
     act = (hidden * cdf).astype(BF)
@@ -112,15 +112,23 @@
     return pl.BlockSpec(shape, lambda *_: (0,) * len(shape))
 
 
-def mlp_half(half, x, cot, vec, bfc, wfc, wproj, carry=None):
+def as_row(ref):
+    return ref[...].reshape(1, ref.shape[0])
+
+
+def in_hbm(*arrays):
+    return [pltpu.with_memory_space_constraint(v, pltpu.HBM) for v in arrays]
+
+
+def mlp_half(half, x, cot, gain, shift, bfc, wfc, wproj, carry=None):
     tok = (SEQ, D)
     in_specs = [
-        whole(tok), whole(tok), whole((8, D)),
-        pl.BlockSpec((1, 256), lambda i, h: (0, h[0] * 3 + i)),
+        whole(tok), whole(tok), whole((D,)), whole((D,)), whole((1, FFL)),
         pl.BlockSpec((D, 256), lambda i, h: (0, h[0] * 3 + i)),
         pl.BlockSpec((256, D), lambda i, h: (h[0] * 3 + i, 0)),
     ]
-    args = [x, cot, vec, bfc, wfc, wproj]
+    x, cot, wfc, wproj = in_hbm(x, cot, wfc, wproj)
+    args = [x, cot, gain, shift, bfc, wfc, wproj]
     if carry is not None:
         in_specs += [whole(tok), whole(tok)]
         args += list(carry)
@@ -153,7 +161,7 @@
 
 
 def attend_kernel(
-    half_ref, x_ref, cot_ref, vec_ref, seg_ref, freq_ref, wq_ref, bq_ref, wo_ref,
+    half_ref, x_ref, cot_ref, g1_ref, b1_ref, g2_ref, seg_ref, freq_ref, wq_ref, bq_ref, wo_ref,
     gm_ref, mo_ref, gb1_ref, gb2_ref,
     grads_ref, n1_ref, gy_ref, out_ref, gx_ref, sm_ref,
     bias, ctab, s1tab, s2tab, gn1, acc,
@@ -164,9 +172,9 @@
     @pl.when(p == 0)
     def _():
         n, _unused = norm_parts(x_ref[...])
-        n1_ref[...] = (n * vec_ref[0:1, :] + vec_ref[1:2, :]).astype(BF)
+        n1_ref[...] = (n * as_row(g1_ref) + as_row(b1_ref)).astype(BF)
         gy_ref[...] = cot_ref[...].astype(BF)
-        seg_row = seg_ref[...]
+        seg_row = as_row(seg_ref).astype(F32)
         seg_col = jnp.transpose(jnp.broadcast_to(seg_row, (128, SEQ)))
         row_at = lax.broadcasted_iota(jnp.int32, (SEQ, 128), 0)
         before = jnp.zeros((SEQ, 128), F32)
@@ -197,7 +205,15 @@
 
     wp = jnp.concatenate([rows(h, part) for part in range(3) for h in range(2)], axis=0)
     n1 = n1_ref[...]
-    mixed = dot_nt(n1, wp) + bq_ref[0]
+    head = lax.broadcasted_iota(jnp.int32, (6, 192), 0)
+    shifts = [
+        jnp.sum(jnp.where(head == 2 * p + h, bq_ref[...], 0.0), axis=0, keepdims=True)
+        for h in range(2)
+    ]
+    shift = jnp.concatenate(
+        [shifts[h][:, part * 64 : part * 64 + 64] for part in range(3) for h in range(2)], axis=1
+    )
+    mixed = dot_nt(n1, wp) + shift
     q = rot(mixed[:, :128], 1.0).astype(BF) * 0.125
     k = rot(mixed[:, 128:256], 1.0).astype(BF)
     v = mixed[:, 256:].astype(BF)
@@ -261,7 +277,7 @@
         out_ref[...] = acc[...].astype(BF)
         n, rstd = norm_parts(x_ref[...])
         u1, u2 = gn1[...], gm_ref[...]
-        ug = u1 * vec_ref[0:1, :] + u2 * vec_ref[2:3, :]
+        ug = u1 * as_row(g1_ref) + u2 * as_row(g2_ref)
         m1 = jnp.mean(ug, axis=-1, keepdims=True)
         m2 = jnp.mean(ug * n, axis=-1, keepdims=True)
         gx_ref[...] = ((ug - m1 - n * m2) * rstd).astype(BF)
@@ -280,17 +296,19 @@
         sm_ref[51:64, :] = jnp.zeros((13, 128), F32)
 
 
-def attend(half, x, cot, vec, seg, freq, wq, bq, wo, gm, mo, gb1, gb2):
+def attend(half, x, cot, g1, b1, g2, seg, freq, wq, bq, wo, gm, mo, gb1, gb2):
     tok = (SEQ, D)
+    x, cot, wq, wo = in_hbm(x, cot, wq, wo)
     return pl.pallas_call(
         attend_kernel,
         grid_spec=pltpu.PrefetchScalarGridSpec(
             num_scalar_prefetch=1,
             grid=(3,),
             in_specs=[
-                whole(tok), whole(tok), whole((8, D)), whole((1, SEQ)), whole((1, 128)),
+                whole(tok), whole(tok), whole((D,)), whole((D,)), whole((D,)), whole((SEQ,)),
+                whole((1, 128)),
                 pl.BlockSpec((384, D), lambda p, h: (p, 0)),
-                pl.BlockSpec((1, 1, 384), lambda p, h: (p, 0, 0)),
+                whole((6, 192)),
                 pl.BlockSpec((128, D), lambda p, h: (p, 0)),
                 whole(tok), whole(tok), whole((1, D)), whole((1, D)),
             ],
@@ -322,7 +340,7 @@
             flops=14 << 30, bytes_accessed=16 << 20, transcendentals=2 << 20
         ),
         name="attend",
-    )(half, x, cot, vec, seg, freq, wq, bq, wo, gm, mo, gb1, gb2)
+    )(half, x, cot, g1, b1, g2, seg, freq, wq, bq, wo, gm, mo, gb1, gb2)
 
 
 def wgrad_kernel(half_ref, g_ref, n1_ref, gy_ref, o_ref):
@@ -366,36 +384,63 @@
     return lax.dynamic_index_in_dim(v, index, axis, keepdims=False)
 
 
-def reduce_chunks(total, pos):
-    a1, a2, z = pos
-    got = [move(total((a1 + d) % 4).astype(BF), FIRST[d]) for d in (1, 3, 2)]
-    own = total(a1)
+class Ordered:
+    def __init__(self):
+        self.token = None
+
+    def __call__(self, fn, *args):
+        if self.token is not None:
+            args, _unused = lax.optimization_barrier((args, self.token))
+        out = fn(*args)
+        self.token = jax.tree.leaves(out)[0]
+        return out
+
+
+def split_first(total, a1):
+    sends = [total((a1 + d) % 4).astype(BF) for d in (1, 3, 2)]
+    return sends, total(a1)
+
+
+def split_second(own, got, a2):
     for g in got:
         own = own + g.astype(F32)
     n, _, w = own.shape
     own = own.reshape(n, 4, 48, w)
-    got = [move(pick(own, (a2 + d) % 4, 1).astype(BF), SECOND[d]) for d in (1, 3, 2)]
-    own = pick(own, a2, 1)
+    return [pick(own, (a2 + d) % 4, 1).astype(BF) for d in (1, 3, 2)], pick(own, a2, 1)
+
+
+def split_z(own, got, z):
     for g in got:
         own = own + g.astype(F32)
+    n, _, w = own.shape
     own = own.reshape(n, 2, 24, w)
-    got = move(pick(own, 1 - z, 1).astype(BF), ZHI)
-    return pick(own, z, 1) + got.astype(F32)
-
-
-def gather_chunks(mine, pos):
-    a1, a2, z = pos
+    return pick(own, 1 - z, 1).astype(BF), pick(own, z, 1)
+
+
+def finish_sum(own, got):
+    return (own + got.astype(F32)).astype(BF)
+
+
+def join_z(mine, other, z):
     n, _, w = mine.shape
-    other = move(mine, ZHI)
     low = jnp.where(z == 0, mine, other)
     high = jnp.where(z == 0, other, mine)
-    part = jnp.stack([low, high], axis=1).reshape(n, 48, w)
-    got = {d: move(part, SECOND[d]) for d in (1, 3, 2)}
-    ring = jnp.stack([part, got[3], got[2], got[1]] + [part, got[3], got[2]], axis=1)
-    chunk = lax.dynamic_slice_in_dim(ring, (4 - a2) % 4, 4, 1).reshape(n, 192, w)
-    got = {d: move(chunk, FIRST[d]) for d in (1, 3, 2)}
-    chunks = [chunk, got[1], got[2], got[3]]
-    return chunks + [move(c, CORE) for c in chunks]
+    return jnp.stack([low, high], axis=1).reshape(n, 48, w)
+
+
+def join_second(part, got, a2):
+    n, _, w = part.shape
+    g1, g3, g2 = got
+    ring = jnp.stack([part, g3, g2, g1, part, g3, g2], axis=1)
+    return lax.dynamic_slice_in_dim(ring, (4 - a2) % 4, 4, 1).reshape(n, 192, w)
+
+
+def send_first(parts):
+    return [move(v, FIRST[d]) for v, d in zip(parts, (1, 3, 2))]
+
+
+def send_second(parts):
+    return [move(v, SECOND[d]) for v, d in zip(parts, (1, 3, 2))]
 
 
 def unpack_mlp_kernel(pos_ref, *refs):
@@ -547,55 +592,105 @@
     keep = core.reshape(1).astype(jnp.int32)
     send = 1 - keep
 
-    bias_sum = b_out + b_proj
-    zero = jnp.zeros_like(ln1_gain)
-    vec = jnp.stack([ln1_gain, ln1_bias, ln2_gain, ln2_bias, bias_sum, zero, zero, zero])
     bfc = b_fc.reshape(1, FFL)
     wq = jnp.transpose(w_qkv, (1, 2, 0)).reshape(1152, D)
     wo = w_out.reshape(384, D)
-    bq = b_qkv.reshape(3, 2, 3, 64).transpose(0, 2, 1, 3).reshape(3, 1, 384)
-    seg = seg_ids.astype(F32).reshape(1, SEQ)
     freq = np.float32(10000.0) ** (np.arange(ROT // 2).astype(np.float32) * np.float32(-2.0 / ROT))
     freq = jnp.asarray(np.tile(freq, 16)[None, :].astype(np.float32))
 
-    gw_send, gm, mo, gb_send = mlp_half(send, layer_input, cotangent, vec, bfc, w_fc, w_proj)
+    run = Ordered()
+    gw_send, gm, mo, gb_send = run(
+        functools.partial(mlp_half, send), layer_input, cotangent, ln2_gain, ln2_bias, bfc, w_fc, w_proj
+    )
     gw_recv = move(gw_send, CORE).reshape(2, 4, 192, D)
-    gw_keep, gm, mo, gb_keep = mlp_half(
-        keep, layer_input, cotangent, vec, bfc, w_fc, w_proj, (gm, mo)
+    gw_keep, gm, mo, gb_keep = run(
+        functools.partial(mlp_half, keep), layer_input, cotangent, ln2_gain, ln2_bias, bfc, w_fc, w_proj, (gm, mo)
     )
     gw_keep = gw_keep.reshape(2, 4, 192, D)
 
-    def mlp_total(j):
-        return pick(gw_keep, j, 1).astype(F32) + pick(gw_recv, j, 1).astype(F32)
-
-    mlp_mine = reduce_chunks(mlp_total, pos).astype(BF)
-
-    grads, n1, gy, out_part, gx_part, small = attend(
-        send, layer_input, cotangent, vec, seg, freq, wq, bq, wo, gm, mo, gb_send, gb_keep
-    )
-    norms = small[:24] + lax.ppermute(small[:24], "tensor", SWAP)
-    small = jnp.concatenate([norms, small[24:]], axis=0)
-    small = small + move(small, CORE)
-    aw_send = wgrad_half(send, grads, n1, gy, "wgrad_send")
+    def mlp_first(kept, recv):
+        return split_first(
+            lambda j: pick(kept, j, 1).astype(F32) + pick(recv, j, 1).astype(F32), a1
+        )
+
+    sends, m_own = run(mlp_first, gw_keep, gw_recv)
+    m_got = send_first(sends)
+
+    grads, n1, gy, out_part, gx_part, small = run(
+        functools.partial(attend, send),
+        layer_input, cotangent, ln1_gain, ln1_bias, ln2_gain, seg_ids, freq, wq, b_qkv, wo, gm, mo, gb_send, gb_keep,
+    )
+    norms_other = lax.ppermute(small[:24], "tensor", SWAP)
+
+    sends, m_own = run(lambda o, g: split_second(o, g, a2), m_own, m_got)
+    m_got = send_second(sends)
+
+    aw_send = run(lambda *v: wgrad_half(send, *v, "wgrad_send"), grads, n1, gy)
     aw_recv = move(aw_send, CORE).reshape(1, 4, 192, D)
-    aw_keep = wgrad_half(keep, grads, n1, gy, "wgrad_keep").reshape(1, 4, 192, D)
-    small_rows = jnp.pad(small, ((0, 128), (0, 0)))[None]
-
-    def attn_total(j):
-        main = pick(aw_keep, j, 1).astype(F32) + pick(aw_recv, j, 1).astype(F32)
-        return jnp.concatenate([main, jnp.where(j == 0, small_rows, 0.0)], axis=2)
-
-    attn_mine = reduce_chunks(attn_total, pos).astype(BF)
-
+
+    m_send, m_own = run(lambda o, g: split_z(o, g, z), m_own, m_got)
+    m_got = move(m_send, ZHI)
+
+    small = run(lambda s, o: jnp.concatenate([s[:24] + o, s[24:]], axis=0), small, norms_other)
+    small_other = move(small, CORE)
+    aw_keep = run(lambda *v: wgrad_half(keep, *v, "wgrad_keep"), grads, n1, gy)
+    aw_keep = aw_keep.reshape(1, 4, 192, D)
+
+    def attn_first(kept, recv, s, o):
+        rows = jnp.pad(s + o, ((0, 128), (0, 0)))[None]
+
+        def total(j):
+            main = pick(kept, j, 1).astype(F32) + pick(recv, j, 1).astype(F32)
+            return jnp.concatenate([main, jnp.where(j == 0, rows, 0.0)], axis=2)
+
+        return split_first(total, a1)
+
+    mine = run(finish_sum, m_own, m_got)
+    m_other = move(mine, ZHI)
+    sends, t_own = run(attn_first, aw_keep, aw_recv, small, small_other)
+    t_got = send_first(sends)
+
+    part = run(lambda m, o: join_z(m, o, z), mine, m_other)
+    m_got = send_second([part] * 3)
+    out_part = run(lambda v: v, out_part)
     out_other = lax.ppermute(out_part, "tensor", SWAP)
+
+    sends, t_own = run(lambda o, g: split_second(o, g, a2), t_own, t_got)
+    t_got = send_second(sends)
+
+    chunk = run(lambda p, g: join_second(p, g, a2), part, m_got)
+    m_got = send_first([chunk] * 3)
+    m_chunks = [chunk, m_got[0], m_got[2], m_got[1]]
+
+    t_send, t_own = run(lambda o, g: split_z(o, g, z), t_own, t_got)
+    t_got = move(t_send, ZHI)
+
+    mine = run(finish_sum, t_own, t_got)
+    t_other = move(mine, ZHI)
+    part = run(lambda m, o: join_z(m, o, z), mine, t_other)
+    t_got = send_second([part] * 3)
+    gx_part = run(lambda v: v, gx_part)
     gx_other = lax.ppermute(gx_part, "tensor", SWAP)
-    output = (
-        layer_input.astype(F32) + (out_part.astype(F32) + out_other.astype(F32)) + bias_sum
-    ).astype(BF)
-    grad_x = cotangent + (gx_part.astype(F32) + gx_other.astype(F32))
-
-    g_proj, g_fc = unpack_mlp(table, gather_chunks(mlp_mine, pos))
-    g_qkv, g_out, sm = unpack_attn(table, gather_chunks(attn_mine, pos))
+
+    chunk = run(lambda p, g: join_second(p, g, a2), part, t_got)
+    t_got = send_first([chunk] * 3)
+    t_chunks = [chunk, t_got[0], t_got[2], t_got[1]]
+
+    output = run(
+        lambda x, p, o: (
+            x.astype(F32) + (p.astype(F32) + o.astype(F32)) + b_out + b_proj
+        ).astype(BF),
+        layer_input, out_part, out_other,
+    )
+
+    m_chunks = m_chunks + [move(v, CORE) for v in m_chunks]
+    g_proj, g_fc = run(lambda *v: unpack_mlp(table, v), *m_chunks)
+    t_chunks = t_chunks + [move(v, CORE) for v in t_chunks]
+    grad_x = run(
+        lambda c, p, o: c + (p.astype(F32) + o.astype(F32)), cotangent, gx_part, gx_other
+    )
+
+    g_qkv, g_out, sm = run(lambda *v: unpack_attn(table, v), *t_chunks)
     g_qkv = jnp.transpose(g_qkv.reshape(6, 192, D), (2, 0, 1))
     g_out = g_out.reshape(6, 64, D)
     vecs = [sm[6 * i : 6 * i + 6].reshape(D) for i in range(5)]

time: 204 us -> 174 us (0.85); the launches traced: 203 us -> 171 us
  starting transfers between devices: 78.9 us -> 56 us
  local copies, waits for them, and re-layouts: 19.4 us -> 11.2 us
  other arithmetic: 13.8 us -> 9.64 us
    ppermute x39, starting transfers between devices: 75.5 us -> 54 us  [move(): return lax.ppermute(v, 'dp', perm)]
    ppermute x1, waiting for transfers between devices: 0.01 us -> 6.76 us  [body(): out_other = lax.ppermute(out_part, 'tensor', SWAP)]
    ppermute x39, waiting for transfers between devices: 40.5 us -> 34.9 us  [move(): return lax.ppermute(v, 'dp', perm)]
    unnamed x71 -> x55, local copies, waits for them, and re-layouts: 12.7 us -> 8.02 us
    add x8 -> x7, other arithmetic: 7.44 us -> 3.04 us  [the longest x1 2.53 us: body(): c + (p.astype(F32) + o.astype(F32))]
    another operation x11 -> x3, local copies, waits for them, and re-layouts: 2.85 us -> 0.04 us  [the longest x2 0.03 us: join_second(): ring = jnp.stack([part, g3, g2, g1, part, g3, g2], axis=1)]
    pallas_call x2, Pallas kernels: 13.2 us -> 15.7 us  [mlp_half(): pl.pallas_call(functools.partial(mlp_kernel, carry is None), grid_spec=pl...]
    convert_element_type x5 -> x4, other arithmetic: 3.85 us -> 6.07 us  [the longest x1 3.36 us: split_first(): sends = [total((a1 + d) % 4).astype(BF) for d in (1, 3, 2)]]
  transfers between devices with their start and end apart: 42 -> 42, of which waited for: 18 -> 9; matrix products, arithmetic and copies ran while one was open for 7% -> 4% of each run, Pallas kernels for 3% -> 23%
where the time goes in v2:
time: 174 us; the launch traced here: 171 us
  starting transfers between devices  56 us (32%)
  Pallas kernels  50.8 us (29%)
  waiting for transfers between devices  41.7 us (24%)
  local copies, waits for them, and re-layouts  11.2 us (6%)
  other arithmetic  9.64 us (6%)
    ppermute x39, starting transfers between devices, move(): return lax.ppermute(v, 'dp', perm)  54 us
    ppermute x39, waiting for transfers between devices, move(): return lax.ppermute(v, 'dp', perm)  34.9 us
    pallas_call x1, Pallas kernels, attend(): pl.pallas_call(attend_kernel, grid_spec=pltpu.PrefetchScalarGridSpec(num_...  20.3 us
    pallas_call x2, Pallas kernels, mlp_half(): pl.pallas_call(functools.partial(mlp_kernel, carry is None), grid_spec=pl...  15.7 us
    unnamed x55, local copies, waits for them, and re-layouts  8.02 us
    ppermute x1, waiting for transfers between devices, body(): out_other = lax.ppermute(out_part, 'tensor', SWAP)  6.76 us
    pallas_call x1, Pallas kernels, unpack_mlp(): pl.pallas_call(unpack_mlp_kernel, grid_spec=pltpu.PrefetchScalarGridSpec(...  6.32 us
    pallas_call x2, Pallas kernels, wgrad_half(): pl.pallas_call(wgrad_kernel, grid_spec=pltpu.PrefetchScalarGridSpec(num_s...  4.43 us
  transfers between devices with their start and end apart: 42, of which 9 were waited for; matrix products, arithmetic and copies ran while one was open for 4% of the time, Pallas kernels for 23%

profile of v2, /device:TPU:1, one launch (start us, length us, event | category | flops | bytes accessed | tf_op | source)
XLA Modules:
  0.0 170.6 jit_solution(18059179574916597746)
XLA Ops:
  0.7 0.7 reshape.382.refs_4_
  1.4 0.7 copy-done.3
  2.0 0.7 copy-done.7
  2.7 7.9 %mlp_send.1 = (bf16[2,768,768]{2,1,0:T(8,128)(2,1)S(1)}, f32[512,768]{1,0:T(8,128)S(1)}, f32[512,768]{1,0:T(8,128)S(1)}, f32[1,768]{1,0:T(1,128)S(1)}) custom-call(s32[1]{0:T(128)S(6)} %sub.42.half_ref, bf16[512,768]{1,0:T(8,128)(2,1)} %x_ref, f32[512,768]{1,0:T(8,128)} %cot_ref, f32[768]{0:T(1024)S(1)} %copy-done.7, f32[768]{0:T(1024)S(1)} %copy-done.3, ...), custom_call_target="tpu_custom_call" | custom-call | flops 3623878656 | bytes 14680064 | tf_op jit(solution)/shard_map/mlp_send/pallas_call | solution.py:135
  10.6 1.1 copy-done.11
  11.8 1.1 copy-done.13
  12.9 1.4 collective-permute-start
  14.3 1.4 copy-done.12
  15.8 1.4 copy-done.14
  17.2 7.9 %mlp_keep.1 = (bf16[2,768,768]{2,1,0:T(8,128)(2,1)S(1)}, f32[512,768]{1,0:T(8,128)S(1)}, f32[512,768]{1,0:T(8,128)S(1)}, f32[1,768]{1,0:T(1,128)S(1)}) custom-call(s32[1]{0:T(128)} %bitcast.half_ref, bf16[512,768]{1,0:T(8,128)(2,1)} %x_ref, f32[512,768]{1,0:T(8,128)} %cot_ref, f32[768]{0:T(1024)S(1)} %copy-done.8, f32[768]{0:T(1024)S(1)} %copy-done.4, ...), custom_call_target="tpu_custom_call" | custom-call | flops 3623878656 | bytes 14680064 | tf_op jit(solution)/shard_map/mlp_keep/pallas_call | solution.py:135
  25.1 3.4 %fusion.2 = (bf16[2,192,768]{2,1,0:T(8,128)(2,1)S(1)}, bf16[2,192,768]{2,1,0:T(8,128)(2,1)S(1)}, f32[2,192,768]{2,1,0:T(8,128)S(1)}, bf16[2,192,768]{2,1,0:T(8,128)(2,1)S(1)}) fusion(s32[]{:T(128)S(6)} %select_n.233, s32[]{:T(128)S(6)} %select_n.231, s32[]{:T(128)S(6)} %select_n.229, s32[]{:T(128)S(6)} %select_n.226, ...), kind=kLoop, calls=%fused_computation.11 | loop fusion | flops 4423680 | bytes 7667728 | tf_op jit(solution)/shard_map/convert_element_type | solution.py:400
  28.5 1.5 collective-permute-start.1
  30.0 2.6 %collective-permute-start.3 = (bf16[2,192,768]{2,1,0:T(8,128)(2,1)S(1)}, bf16[2,192,768]{2,1,0:T(8,128)(2,1)S(1)}, u32[]{:S(2)}, u32[]{:S(2)}) collective-permute-start(bf16[2,192,768]{2,1,0:T(8,128)(2,1)S(1)} %get-tuple-element.238), channel_id=1, source_target_pairs={{0,32},{2,10},{4,36},{6,14},{8,40},{10,2},{12,44},{14,6},{16,48},{... | collective-permute-start | bytes 1769480 | tf_op jit(solution)/shard_map/ppermute | solution.py:52
  32.6 1.1 collective-permute-start.2
  33.7 20.3 %attend.1 = (bf16[512,1536]{1,0:T(8,128)(2,1)S(1)}, bf16[512,768]{1,0:T(8,128)(2,1)S(1)}, bf16[512,768]{1,0:T(8,128)(2,1)S(1)}, bf16[512,768]{1,0:T(8,128)(2,1)S...) custom-call(s32[1]{0:T(128)S(6)} %sub.42.half_ref, bf16[512,768]{1,0:T(8,128)(2,1)} %x_ref, f32[512,768]{1,0:T(8,128)} %cot_ref, ...), custom_call_target="tpu_custom_call" | custom-call | flops 15032385536 | bytes 16777216 | tf_op jit(solution)/shard_map/attend/pallas_call | solution.py:302
  54.0 1.7 %collective-permute-start.8 = (f32[24,128]{1,0:T(8,128)S(1)}, f32[24,128]{1,0:T(8,128)S(1)}, u32[]{:S(2)}, u32[]{:S(2)}) collective-permute-start(f32[24,128]{1,0:T(8,128)S(1)} %slice.30), channel_id=1, source_target_pairs={{0,1},{1,0},{2,3},{3,2},{4,5},{5,4},{6,7},{7,6},{8,9},{9,8},{10,11... | collective-permute-start | bytes 36872 | tf_op jit(solution)/shard_map/ppermute | solution.py:623
  56.1 1.3 collective-permute-start.4
  57.3 2.5 %collective-permute-start.6 = (bf16[2,48,768]{2,1,0:T(8,128)(2,1)S(1)}, bf16[2,48,768]{2,1,0:T(8,128)(2,1)S(1)}, u32[]{:S(2)}, u32[]{:S(2)}) collective-permute-start(bf16[2,48,768]{2,1,0:T(8,128)(2,1)S(1)} %get-tuple-element.246), channel_id=1, source_target_pairs={{0,8},{2,34},{4,12},{6,38},{8,0},{10,42},{12,4},{14,46},{16,24},{1... | collective-permute-start | bytes 442376 | tf_op jit(solution)/shard_map/ppermute | solution.py:52
  59.8 1.2 collective-permute-start.5
  61.0 2.2 %wgrad_send.1 = bf16[768,768]{1,0:T(8,128)(2,1)S(1)} custom-call(s32[1]{0:T(128)S(6)} %sub.42.half_ref, bf16[512,1536]{1,0:T(8,128)(2,1)S(1)} %get-tuple-element.177.g_ref, bf16[512,768]{1,0:T(8,128)(2,1)S(1)} %get-tuple-element.178.n1_ref, bf16[512,768]{1,0:T(8,128)(2,1)S(1)} %get-tuple-element.179.gy_ref), custom_call_target="tpu_custom_call" | custom-call | flops 603979776 | bytes 4194304 | tf_op jit(solution)/shard_map/wgrad_send/pallas_call | solution.py:361
  63.2 2.0 %collective-permute-start.10 = (bf16[768,768]{1,0:T(8,128)(2,1)S(1)}, bf16[768,768]{1,0:T(8,128)(2,1)S(1)}, u32[]{:S(2)}, u32[]{:S(2)}) collective-permute-start(bf16[768,768]{1,0:T(8,128)(2,1)S(1)} %wgrad_send.1), channel_id=1, source_target_pairs={{0,2},{2,0},{4,6},{6,4},{8,10},{10,8},{12,14},{14,12},{16,18},{18,... | collective-permute-start | bytes 3538952 | tf_op jit(solution)/shard_map/ppermute | solution.py:52
  65.4 3.4 %collective-permute-start.7 = (bf16[2,24,768]{2,1,0:T(8,128)(2,1)S(1)}, bf16[2,24,768]{2,1,0:T(8,128)(2,1)S(1)}, u32[]{:S(2)}, u32[]{:S(2)}) collective-permute-start(bf16[2,24,768]{2,1,0:T(8,128)(2,1)S(1)} %fusion.16), channel_id=1, source_target_pairs={{0,64},{2,66},{4,68},{6,70},{8,72},{10,74},{12,76},{14,78},{16,80}... | collective-permute-start | bytes 221192 | tf_op jit(solution)/shard_map/ppermute | solution.py:52
  68.8 1.8 %collective-permute-start.11 = (f32[64,128]{1,0:T(8,128)S(1)}, f32[64,128]{1,0:T(8,128)S(1)}, u32[]{:S(2)}, u32[]{:S(2)}) collective-permute-start(f32[64,128]{1,0:T(8,128)S(1)} %pad_maximum_fusion.6), channel_id=1, source_target_pairs={{0,2},{2,0},{4,6},{6,4},{8,10},{10,8},{12,14},{14,12},{16,18},{18,... | collective-permute-start | bytes 98312 | tf_op jit(solution)/shard_map/ppermute | solution.py:52
  70.6 2.2 %wgrad_keep.1 = bf16[768,768]{1,0:T(8,128)(2,1)S(1)} custom-call(s32[1]{0:T(128)} %bitcast.half_ref, bf16[512,1536]{1,0:T(8,128)(2,1)S(1)} %get-tuple-element.177.g_ref, bf16[512,768]{1,0:T(8,128)(2,1)S(1)} %get-tuple-element.178.n1_ref, bf16[512,768]{1,0:T(8,128)(2,1)S(1)} %get-tuple-element.179.gy_ref), custom_call_target="tpu_custom_call" | custom-call | flops 603979776 | bytes 4194304 | tf_op jit(solution)/shard_map/wgrad_keep/pallas_call | solution.py:361
  72.8 0.9 collective-permute-start.9
  73.8 0.3 fusion.5
  74.2 0.5 collective-permute-start.13
  74.6 3.9 %collective-permute-done.9 = bf16[2,24,768]{2,1,0:T(8,128)(2,1)S(1)} collective-permute-done((bf16[2,24,768]{2,1,0:T(8,128)(2,1)S(1)}, bf16[2,24,768]{2,1,0:T(8,128)(2,1)S(1)}, u32[]{:S(2)}, u32[]{:S(2)}) %collective-permute-start.9) | collective-permute-done | bytes 73760 | tf_op jit(solution)/shard_map/ppermute | solution.py:52
  78.5 2.3 %collective-permute-start.14 = (bf16[1,192,896]{2,1,0:T(8,128)(2,1)S(1)}, bf16[1,192,896]{2,1,0:T(8,128)(2,1)S(1)}, u32[]{:S(2)}, u32[]{:S(2)}) collective-permute-start(bf16[1,192,896]{2,1,0:T(8,128)(2,1)S(1)} %pad_maximum_fusion.2), channel_id=1, source_target_pairs={{0,48},{2,14},{4,52},{6,2},{8,56},{10,6},{12,60},{14,10},{16,0},{1... | collective-permute-start | bytes 1032200 | tf_op jit(solution)/shard_map/ppermute | solution.py:52
  80.9 0.5 collective-permute-start.15
  81.5 0.3 collective-permute-start.21
  81.8 2.5 %collective-permute-start.20 = (bf16[2,48,768]{2,1,0:T(8,128)(2,1)S(1)}, bf16[2,48,768]{2,1,0:T(8,128)(2,1)S(1)}, u32[]{:S(2)}, u32[]{:S(2)}) collective-permute-start(bf16[2,48,768]{2,1,0:T(8,128)(2,1)S(1)} %bitcast.148), channel_id=1, source_target_pairs={{0,12},{2,50},{4,0},{6,54},{8,4},{10,58},{12,8},{14,62},{16,28},{1... | collective-permute-start | bytes 442376 | tf_op jit(solution)/shard_map/ppermute | solution.py:52
  84.3 6.9 %collective-permute-done.14 = bf16[1,192,896]{2,1,0:T(8,128)(2,1)S(1)} collective-permute-done((bf16[1,192,896]{2,1,0:T(8,128)(2,1)S(1)}, bf16[1,192,896]{2,1,0:T(8,128)(2,1)S(1)}, u32[]{:S(2)}, u32[]{:S(2)}) %collective-permute-start.14) | collective-permute-done | bytes 344096 | tf_op jit(solution)/shard_map/ppermute | solution.py:52
  91.8 4.9 %collective-permute-done.19 = bf16[2,48,768]{2,1,0:T(8,128)(2,1)S(1)} collective-permute-done((bf16[2,48,768]{2,1,0:T(8,128)(2,1)S(1)}, bf16[2,48,768]{2,1,0:T(8,128)(2,1)S(1)}, u32[]{:S(2)}, u32[]{:S(2)}) %collective-permute-start.19) | collective-permute-done | bytes 147488 | tf_op jit(solution)/shard_map/ppermute | solution.py:52
  96.7 1.1 collective-permute-start.17
  98.1 3.7 %collective-permute-done.18 = bf16[1,48,896]{2,1,0:T(8,128)(2,1)S(1)} collective-permute-done((bf16[1,48,896]{2,1,0:T(8,128)(2,1)S(1)}, bf16[1,48,896]{2,1,0:T(8,128)(2,1)S(1)}, u32[]{:S(2)}, u32[]{:S(2)}) %collective-permute-start.18) | collective-permute-done | bytes 86048 | tf_op jit(solution)/shard_map/ppermute | solution.py:52
  102.0 4.3 %collective-permute-done.22 = bf16[1,24,896]{2,1,0:T(8,128)(2,1)S(1)} collective-permute-done((bf16[1,24,896]{2,1,0:T(8,128)(2,1)S(1)}, bf16[1,24,896]{2,1,0:T(8,128)(2,1)S(1)}, u32[]{:S(2)}, u32[]{:S(2)}) %collective-permute-start.22) | collective-permute-done | bytes 43040 | tf_op jit(solution)/shard_map/ppermute | solution.py:52
  106.5 4.4 %collective-permute-done.23 = bf16[1,24,896]{2,1,0:T(8,128)(2,1)S(1)} collective-permute-done((bf16[1,24,896]{2,1,0:T(8,128)(2,1)S(1)}, bf16[1,24,896]{2,1,0:T(8,128)(2,1)S(1)}, u32[]{:S(2)}, u32[]{:S(2)}) %collective-permute-start.23) | collective-permute-done | bytes 43040 | tf_op jit(solution)/shard_map/ppermute | solution.py:52
  110.9 1.3 collective-permute-start.26
  112.2 0.6 collective-permute-start.25
  112.8 0.9 collective-permute-start.24
  113.7 4.4 %collective-permute-start.31 = (bf16[2,192,768]{2,1,0:T(8,128)(2,1)S(1)}, bf16[2,192,768]{2,1,0:T(8,128)(2,1)S(1)}, u32[]{:S(2)}, u32[]{:S(2)}) collective-permute-start(bf16[2,192,768]{2,1,0:T(8,128)(2,1)S(1)} %bitcast.132), channel_id=1, source_target_pairs={{0,2},{2,0},{4,6},{6,4},{8,10},{10,8},{12,14},{14,12},{16,18},{18,... | collective-permute-start | bytes 1769480 | tf_op jit(solution)/shard_map/ppermute | solution.py:52
  118.1 2.7 %collective-permute-start.30 = (bf16[2,192,768]{2,1,0:T(8,128)(2,1)S(1)}, bf16[2,192,768]{2,1,0:T(8,128)(2,1)}, u32[]{:S(2)}, u32[]{:S(2)}) collective-permute-start(bf16[2,192,768]{2,1,0:T(8,128)(2,1)S(1)} %bitcast.133), channel_id=1, source_target_pairs={{0,48},{2,14},{4,52},{6,2},{8,56},{10,6},{12,60},{14,10},{16,0},{1... | collective-permute-start | bytes 1769480 | tf_op jit(solution)/shard_map/ppermute | solution.py:52
  120.8 0.7 collective-permute-start.28
  121.6 6.8 %collective-permute-done.12 = bf16[512,768]{1,0:T(8,128)(2,1)} collective-permute-done((bf16[512,768]{1,0:T(8,128)(2,1)S(1)}, bf16[512,768]{1,0:T(8,128)(2,1)}, u32[]{:S(2)}, u32[]{:S(2)}) %collective-permute-start.12) | collective-permute-done | bytes 786464 | tf_op jit(solution)/shard_map/ppermute | solution.py:656
  128.4 4.2 %collective-permute-start.37 = (bf16[1,192,896]{2,1,0:T(8,128)(2,1)S(1)}, bf16[1,192,896]{2,1,0:T(8,128)(2,1)S(1)}, u32[]{:S(2)}, u32[]{:S(2)}) collective-permute-start(bf16[1,192,896]{2,1,0:T(8,128)(2,1)S(1)} %bitcast.138), channel_id=1, source_target_pairs={{0,48},{2,14},{4,52},{6,2},{8,56},{10,6},{12,60},{14,10},{16,0},{1... | collective-permute-start | bytes 1032200 | tf_op jit(solution)/shard_map/ppermute | solution.py:52
  132.6 0.3 collective-permute-start.27
  132.9 1.0 collective-permute-done.30.refs_3_
  133.9 5.9 %collective-permute-start.34 = (bf16[2,192,768]{2,1,0:T(8,128)(2,1)}, bf16[2,192,768]{2,1,0:T(8,128)(2,1)}, u32[]{:S(2)}, u32[]{:S(2)}) collective-permute-start(bf16[2,192,768]{2,1,0:T(8,128)(2,1)} %collective-permute-done.30.refs_3_), channel_id=1, source_target_pairs={{0,2},{2,0},{4,6},{6,4},{8,10},{10,8},{12,14},{14,12},{16,18},{18,... | collective-permute-start | bytes 1769480 | tf_op jit(solution)/shard_map/ppermute | solution.py:52
  139.8 0.6 collective-permute-start.33
  140.3 1.5 collective-permute-start.32
  141.9 0.7 copy-done
  142.6 2.6 %collective-permute-start.35 = (bf16[1,192,896]{2,1,0:T(8,128)(2,1)S(1)}, bf16[1,192,896]{2,1,0:T(8,128)(2,1)}, u32[]{:S(2)}, u32[]{:S(2)}) collective-permute-start(bf16[1,192,896]{2,1,0:T(8,128)(2,1)S(1)} %bitcast.140), channel_id=1, source_target_pairs={{0,16},{2,6},{4,20},{6,10},{8,24},{10,14},{12,28},{14,2},{16,32},{... | collective-permute-start | bytes 1032200 | tf_op jit(solution)/shard_map/ppermute | solution.py:52
  145.3 2.7 %add_convert_fusion = bf16[512,768]{1,0:T(8,128)(2,1)} fusion(bf16[512,768]{1,0:T(8,128)(2,1)} %collective-permute-done.12, bf16[512,768]{1,0:T(8,128)(2,1)S(1)} %get-tuple-element.212, bf16[512,768]{1,0:T(8,128)(2,1)} %x_ref, f32[768]{0:T(1024)S(1)} %copy-done.19, f32[768]{0:T(1024)S(1)} %copy-done.20), kind=kLoop, calls=%fused_computation.1 | loop fusion | flops 3145728 | bytes 3151872 | tf_op jit(solution)/shard_map/convert_element_type | solution.py:682
  148.0 5.7 %collective-permute-done.35.refs_1_ = bf16[1,192,896]{2,1,0:T(8,128)(2,1)} collective-permute-done((bf16[1,192,896]{2,1,0:T(8,128)(2,1)S(1)}, bf16[1,192,896]{2,1,0:T(8,128)(2,1)}, u32[]{:S(2)}, u32[]{:S(2)}) %collective-permute-start.35) | collective-permute-done | bytes 344096 | tf_op jit(solution)/shard_map/ppermute | solution.py:52
  153.7 0.9 collective-permute-start.38
  154.6 0.5 collective-permute-start.40
  155.2 6.3 %unpack_mlp.1 = (f32[1536,768]{1,0:T(8,128)}, f32[768,1536]{1,0:T(8,128)}) custom-call(s32[16]{0:T(128)S(1)} %stack.116.pos_ref, bf16[2,192,768]{2,1,0:T(8,128)(2,1)S(1)} %bitcast.136, bf16[2,192,768]{2,1,0:T(8,128)(2,1)} %collective-permute-done.28.refs_1_, bf16[2,192,768]{2,1,0:T(8,128)(2,1)} %collective-permute-done.29.refs_2_, ...), custom_call_target="tpu_custom_call" | custom-call | bytes 14680064 | tf_op jit(solution)/shard_map/unpack_mlp/pallas_call | solution.py:470
  161.5 2.5 %add_add_fusion = f32[512,768]{1,0:T(8,128)} fusion(f32[512,768]{1,0:T(8,128)S(1)} %copy-done.17, bf16[512,768]{1,0:T(8,128)(2,1)} %collective-permute-done.27, bf16[512,768]{1,0:T(8,128)(2,1)S(1)} %get-tuple-element.224), kind=kLoop, calls=%fused_computation | loop fusion | flops 1572864 | bytes 4718592 | tf_op jit(solution)/shard_map/add | solution.py:690
  164.1 3.9 %unpack_attn.1 = (f32[1152,768]{1,0:T(8,128)}, f32[384,768]{1,0:T(8,128)}, f32[64,128]{1,0:T(8,128)S(1)}) custom-call(s32[16]{0:T(128)S(1)} %stack.116.pos_ref, bf16[1,192,896]{2,1,0:T(8,128)(2,1)S(1)} %bitcast.142, bf16[1,192,896]{2,1,0:T(8,128)(2,1)} %collective-permute-done.35.refs_1_, bf16[1,192,896]{2,1,0:T(8,128)(2,1)S(1)} %copy-done.1, ...), custom_call_target="tpu_custom_call" | custom-call | bytes 8388608 | tf_op jit(solution)/shard_map/unpack_attn/pallas_call | solution.py:548
  168.0 0.6 slice_bitcast_fusion
  168.6 0.6 slice_bitcast_fusion.1
  169.3 0.7 reshape.401
  170.0 0.6 copy.91
  (129 shorter events, 2.2 us)
Async XLA Ops:
  1.4 0.7 copy-start.3
  2.0 0.7 copy-start.7
  2.7 11.6 %copy-start.4 = (f32[768]{0:T(1024)S(1)}, f32[768]{0:T(1024)}, u32[]{:S(2)}) copy-start(f32[768]{0:T(1024)} %refs_3_.2) | copy-start | bytes 9220
  2.7 11.6 %copy-start.8 = (f32[768]{0:T(1024)S(1)}, f32[768]{0:T(1024)}, u32[]{:S(2)}) copy-start(f32[768]{0:T(1024)} %g2_ref) | copy-start | bytes 9220
  10.6 1.1 copy-start.11
  11.8 1.1 copy-start.13
  12.9 12.1 %collective-permute-start = (bf16[2,768,768]{2,1,0:T(8,128)(2,1)S(1)}, bf16[2,768,768]{2,1,0:T(8,128)(2,1)}, u32[]{:S(2)}, u32[]{:S(2)}) collective-permute-start(bf16[2,768,768]{2,1,0:T(8,128)(2,1)S(1)} %get-tuple-element.128), channel_id=1, source_target_pairs={{0,2},{2,0},{4,6},{6,4},{8,10},{10,8},{12,14},{14,12},{16,18},{18,... | collective-permute-start | bytes 7077896 | tf_op jit(solution)/shard_map/ppermute | solution.py:52
  14.3 1.4 copy-start.12
  15.8 1.4 copy-start.14
  25.0 3.5 %copy-start.15 = (f32[512,768]{1,0:T(8,128)}, f32[512,768]{1,0:T(8,128)S(1)}, u32[]{:S(2)}) copy-start(f32[512,768]{1,0:T(8,128)S(1)} %get-tuple-element.155.gm_ref) | copy-start | bytes 4718596
  25.0 3.5 %copy-start.16 = (f32[512,768]{1,0:T(8,128)}, f32[512,768]{1,0:T(8,128)S(1)}, u32[]{:S(2)}) copy-start(f32[512,768]{1,0:T(8,128)S(1)} %get-tuple-element.156.mo_ref) | copy-start | bytes 4718596
  25.1 8.6 %copy-start.2 = (f32[6,192]{1,0:T(8,128)S(1)}, f32[6,192]{1,0:T(8,128)}, u32[]{:S(2)}) copy-start(f32[6,192]{1,0:T(8,128)} %bq_ref) | copy-start | bytes 13828
  25.1 8.6 %copy-start.5 = (f32[768]{0:T(1024)S(1)}, f32[768]{0:T(1024)}, u32[]{:S(2)}) copy-start(f32[768]{0:T(1024)} %g1_ref) | copy-start | bytes 9220
  25.1 8.6 %copy-start.6 = (f32[768]{0:T(1024)S(1)}, f32[768]{0:T(1024)}, u32[]{:S(2)}) copy-start(f32[768]{0:T(1024)} %b1_ref) | copy-start | bytes 9220
  25.1 8.6 %copy-start.9 = (s32[512]{0:T(512)S(1)}, s32[512]{0:T(512)}, u32[]{:S(2)}) copy-start(s32[512]{0:T(512)} %seg_ref) | copy-start | bytes 6148
  25.1 8.6 %copy-start.10 = (f32[1,128]{1,0:T(1,128)S(1)}, f32[1,128]{1,0:T(1,128)}, u32[]{:S(2)}) copy-start(f32[1,128]{1,0:T(1,128)} %constant.227.clone.freq_ref) | copy-start | bytes 1540
  28.5 27.2 %collective-permute-start.1 = (bf16[2,192,768]{2,1,0:T(8,128)(2,1)S(1)}, bf16[2,192,768]{2,1,0:T(8,128)(2,1)S(1)}, u32[]{:S(2)}, u32[]{:S(2)}) collective-permute-start(bf16[2,192,768]{2,1,0:T(8,128)(2,1)S(1)} %get-tuple-element.241), channel_id=1, source_target_pairs={{0,16},{2,6},{4,20},{6,10},{8,24},{10,14},{12,28},{14,2},{16,32},{... | collective-permute-start | bytes 1769480 | tf_op jit(solution)/shard_map/ppermute | solution.py:52
  30.0 25.8 %collective-permute-start.3 = (bf16[2,192,768]{2,1,0:T(8,128)(2,1)S(1)}, bf16[2,192,768]{2,1,0:T(8,128)(2,1)S(1)}, u32[]{:S(2)}, u32[]{:S(2)}) collective-permute-start(bf16[2,192,768]{2,1,0:T(8,128)(2,1)S(1)} %get-tuple-element.238), channel_id=1, source_target_pairs={{0,32},{2,10},{4,36},{6,14},{8,40},{10,2},{12,44},{14,6},{16,48},{... | collective-permute-start | bytes 1769480 | tf_op jit(solution)/shard_map/ppermute | solution.py:52
  32.6 23.2 %collective-permute-start.2 = (bf16[2,192,768]{2,1,0:T(8,128)(2,1)S(1)}, bf16[2,192,768]{2,1,0:T(8,128)(2,1)S(1)}, u32[]{:S(2)}, u32[]{:S(2)}) collective-permute-start(bf16[2,192,768]{2,1,0:T(8,128)(2,1)S(1)} %get-tuple-element.239), channel_id=1, source_target_pairs={{0,48},{2,14},{4,52},{6,2},{8,56},{10,6},{12,60},{14,10},{16,0},{1... | collective-permute-start | bytes 1769480 | tf_op jit(solution)/shard_map/ppermute | solution.py:52
  54.0 14.7 %collective-permute-start.8 = (f32[24,128]{1,0:T(8,128)S(1)}, f32[24,128]{1,0:T(8,128)S(1)}, u32[]{:S(2)}, u32[]{:S(2)}) collective-permute-start(f32[24,128]{1,0:T(8,128)S(1)} %slice.30), channel_id=1, source_target_pairs={{0,1},{1,0},{2,3},{3,2},{4,5},{5,4},{6,7},{7,6},{8,9},{9,8},{10,11... | collective-permute-start | bytes 36872 | tf_op jit(solution)/shard_map/ppermute | solution.py:623
  56.1 9.2 %collective-permute-start.4 = (bf16[2,48,768]{2,1,0:T(8,128)(2,1)S(1)}, bf16[2,48,768]{2,1,0:T(8,128)(2,1)S(1)}, u32[]{:S(2)}, u32[]{:S(2)}) collective-permute-start(bf16[2,48,768]{2,1,0:T(8,128)(2,1)S(1)} %get-tuple-element.247), channel_id=1, source_target_pairs={{0,4},{2,18},{4,8},{6,22},{8,12},{10,26},{12,0},{14,30},{16,20},{1... | collective-permute-start | bytes 442376 | tf_op jit(solution)/shard_map/ppermute | solution.py:52
  57.3 7.9 %collective-permute-start.6 = (bf16[2,48,768]{2,1,0:T(8,128)(2,1)S(1)}, bf16[2,48,768]{2,1,0:T(8,128)(2,1)S(1)}, u32[]{:S(2)}, u32[]{:S(2)}) collective-permute-start(bf16[2,48,768]{2,1,0:T(8,128)(2,1)S(1)} %get-tuple-element.246), channel_id=1, source_target_pairs={{0,8},{2,34},{4,12},{6,38},{8,0},{10,42},{12,4},{14,46},{16,24},{1... | collective-permute-start | bytes 442376 | tf_op jit(solution)/shard_map/ppermute | solution.py:52
  59.8 5.5 %collective-permute-start.5 = (bf16[2,48,768]{2,1,0:T(8,128)(2,1)S(1)}, bf16[2,48,768]{2,1,0:T(8,128)(2,1)S(1)}, u32[]{:S(2)}, u32[]{:S(2)}) collective-permute-start(bf16[2,48,768]{2,1,0:T(8,128)(2,1)S(1)} %get-tuple-element.248), channel_id=1, source_target_pairs={{0,12},{2,50},{4,0},{6,54},{8,4},{10,58},{12,8},{14,62},{16,28},{1... | collective-permute-start | bytes 442376 | tf_op jit(solution)/shard_map/ppermute | solution.py:52
  63.2 10.6 %collective-permute-start.10 = (bf16[768,768]{1,0:T(8,128)(2,1)S(1)}, bf16[768,768]{1,0:T(8,128)(2,1)S(1)}, u32[]{:S(2)}, u32[]{:S(2)}) collective-permute-start(bf16[768,768]{1,0:T(8,128)(2,1)S(1)} %wgrad_send.1), channel_id=1, source_target_pairs={{0,2},{2,0},{4,6},{6,4},{8,10},{10,8},{12,14},{14,12},{16,18},{18,... | collective-permute-start | bytes 3538952 | tf_op jit(solution)/shard_map/ppermute | solution.py:52
  65.4 7.4 %collective-permute-start.7 = (bf16[2,24,768]{2,1,0:T(8,128)(2,1)S(1)}, bf16[2,24,768]{2,1,0:T(8,128)(2,1)S(1)}, u32[]{:S(2)}, u32[]{:S(2)}) collective-permute-start(bf16[2,24,768]{2,1,0:T(8,128)(2,1)S(1)} %fusion.16), channel_id=1, source_target_pairs={{0,64},{2,66},{4,68},{6,70},{8,72},{10,74},{12,76},{14,78},{16,80}... | collective-permute-start | bytes 221192 | tf_op jit(solution)/shard_map/ppermute | solution.py:52
  68.8 5.0 %collective-permute-start.11 = (f32[64,128]{1,0:T(8,128)S(1)}, f32[64,128]{1,0:T(8,128)S(1)}, u32[]{:S(2)}, u32[]{:S(2)}) collective-permute-start(f32[64,128]{1,0:T(8,128)S(1)} %pad_maximum_fusion.6), channel_id=1, source_target_pairs={{0,2},{2,0},{4,6},{6,4},{8,10},{10,8},{12,14},{14,12},{16,18},{18,... | collective-permute-start | bytes 98312 | tf_op jit(solution)/shard_map/ppermute | solution.py:52
  72.8 5.7 %collective-permute-start.9 = (bf16[2,24,768]{2,1,0:T(8,128)(2,1)S(1)}, bf16[2,24,768]{2,1,0:T(8,128)(2,1)S(1)}, u32[]{:S(2)}, u32[]{:S(2)}) collective-permute-start(bf16[2,24,768]{2,1,0:T(8,128)(2,1)S(1)} %add_convert_fusion.7), channel_id=1, source_target_pairs={{0,64},{2,66},{4,68},{6,70},{8,72},{10,74},{12,76},{14,78},{16,80}... | collective-permute-start | bytes 221192 | tf_op jit(solution)/shard_map/ppermute | solution.py:52
  74.2 17.3 %collective-permute-start.13 = (bf16[1,192,896]{2,1,0:T(8,128)(2,1)S(1)}, bf16[1,192,896]{2,1,0:T(8,128)(2,1)S(1)}, u32[]{:S(2)}, u32[]{:S(2)}) collective-permute-start(bf16[1,192,896]{2,1,0:T(8,128)(2,1)S(1)} %pad_maximum_fusion.1), channel_id=1, source_target_pairs={{0,16},{2,6},{4,20},{6,10},{8,24},{10,14},{12,28},{14,2},{16,32},{... | collective-permute-start | bytes 1032200 | tf_op jit(solution)/shard_map/ppermute | solution.py:52
  78.5 12.7 %collective-permute-start.14 = (bf16[1,192,896]{2,1,0:T(8,128)(2,1)S(1)}, bf16[1,192,896]{2,1,0:T(8,128)(2,1)S(1)}, u32[]{:S(2)}, u32[]{:S(2)}) collective-permute-start(bf16[1,192,896]{2,1,0:T(8,128)(2,1)S(1)} %pad_maximum_fusion.2), channel_id=1, source_target_pairs={{0,48},{2,14},{4,52},{6,2},{8,56},{10,6},{12,60},{14,10},{16,0},{1... | collective-permute-start | bytes 1032200 | tf_op jit(solution)/shard_map/ppermute | solution.py:52
  80.9 10.6 %collective-permute-start.15 = (bf16[1,192,896]{2,1,0:T(8,128)(2,1)S(1)}, bf16[1,192,896]{2,1,0:T(8,128)(2,1)S(1)}, u32[]{:S(2)}, u32[]{:S(2)}) collective-permute-start(bf16[1,192,896]{2,1,0:T(8,128)(2,1)S(1)} %pad_maximum_fusion.3), channel_id=1, source_target_pairs={{0,32},{2,10},{4,36},{6,14},{8,40},{10,2},{12,44},{14,6},{16,48},{... | collective-permute-start | bytes 1032200 | tf_op jit(solution)/shard_map/ppermute | solution.py:52
  81.5 10.3 %collective-permute-start.21 = (bf16[2,48,768]{2,1,0:T(8,128)(2,1)S(1)}, bf16[2,48,768]{2,1,0:T(8,128)(2,1)S(1)}, u32[]{:S(2)}, u32[]{:S(2)}) collective-permute-start(bf16[2,48,768]{2,1,0:T(8,128)(2,1)S(1)} %bitcast.147), channel_id=1, source_target_pairs={{0,8},{2,34},{4,12},{6,38},{8,0},{10,42},{12,4},{14,46},{16,24},{1... | collective-permute-start | bytes 442376 | tf_op jit(solution)/shard_map/ppermute | solution.py:52
  81.8 10.0 %collective-permute-start.20 = (bf16[2,48,768]{2,1,0:T(8,128)(2,1)S(1)}, bf16[2,48,768]{2,1,0:T(8,128)(2,1)S(1)}, u32[]{:S(2)}, u32[]{:S(2)}) collective-permute-start(bf16[2,48,768]{2,1,0:T(8,128)(2,1)S(1)} %bitcast.148), channel_id=1, source_target_pairs={{0,12},{2,50},{4,0},{6,54},{8,4},{10,58},{12,8},{14,62},{16,28},{1... | collective-permute-start | bytes 442376 | tf_op jit(solution)/shard_map/ppermute | solution.py:52
  91.3 5.5 %collective-permute-start.19 = (bf16[2,48,768]{2,1,0:T(8,128)(2,1)S(1)}, bf16[2,48,768]{2,1,0:T(8,128)(2,1)S(1)}, u32[]{:S(2)}, u32[]{:S(2)}) collective-permute-start(bf16[2,48,768]{2,1,0:T(8,128)(2,1)S(1)} %bitcast.149), channel_id=1, source_target_pairs={{0,4},{2,18},{4,8},{6,22},{8,12},{10,26},{12,0},{14,30},{16,20},{1... | collective-permute-start | bytes 442376 | tf_op jit(solution)/shard_map/ppermute | solution.py:52
  91.7 10.1 %collective-permute-start.16 = (bf16[1,48,896]{2,1,0:T(8,128)(2,1)S(1)}, bf16[1,48,896]{2,1,0:T(8,128)(2,1)S(1)}, u32[]{:S(2)}, u32[]{:S(2)}) collective-permute-start(bf16[1,48,896]{2,1,0:T(8,128)(2,1)S(1)} %get-tuple-element.251), channel_id=1, source_target_pairs={{0,4},{2,18},{4,8},{6,22},{8,12},{10,26},{12,0},{14,30},{16,20},{1... | collective-permute-start | bytes 258056 | tf_op jit(solution)/shard_map/ppermute | solution.py:52
  96.7 5.1 %collective-permute-start.18 = (bf16[1,48,896]{2,1,0:T(8,128)(2,1)S(1)}, bf16[1,48,896]{2,1,0:T(8,128)(2,1)S(1)}, u32[]{:S(2)}, u32[]{:S(2)}) collective-permute-start(bf16[1,48,896]{2,1,0:T(8,128)(2,1)S(1)} %get-tuple-element.249), channel_id=1, source_target_pairs={{0,8},{2,34},{4,12},{6,38},{8,0},{10,42},{12,4},{14,46},{16,24},{1... | collective-permute-start | bytes 258056 | tf_op jit(solution)/shard_map/ppermute | solution.py:52
  96.7 5.1 %collective-permute-start.17 = (bf16[1,48,896]{2,1,0:T(8,128)(2,1)S(1)}, bf16[1,48,896]{2,1,0:T(8,128)(2,1)S(1)}, u32[]{:S(2)}, u32[]{:S(2)}) collective-permute-start(bf16[1,48,896]{2,1,0:T(8,128)(2,1)S(1)} %get-tuple-element.250), channel_id=1, source_target_pairs={{0,12},{2,50},{4,0},{6,54},{8,4},{10,58},{12,8},{14,62},{16,28},{1... | collective-permute-start | bytes 258056 | tf_op jit(solution)/shard_map/ppermute | solution.py:52
  101.9 43.4 %copy-start.19 = (f32[768]{0:T(1024)S(1)}, f32[768]{0:T(1024)}, u32[]{:S(2)}) copy-start(f32[768]{0:T(1024)} %param.29) | copy-start | bytes 9220
  101.9 43.4 %copy-start.20 = (f32[768]{0:T(1024)S(1)}, f32[768]{0:T(1024)}, u32[]{:S(2)}) copy-start(f32[768]{0:T(1024)} %param.25) | copy-start | bytes 9220
  101.9 4.5 %collective-permute-start.22 = (bf16[1,24,896]{2,1,0:T(8,128)(2,1)S(1)}, bf16[1,24,896]{2,1,0:T(8,128)(2,1)S(1)}, u32[]{:S(2)}, u32[]{:S(2)}) collective-permute-start(bf16[1,24,896]{2,1,0:T(8,128)(2,1)S(1)} %fusion.20), channel_id=1, source_target_pairs={{0,64},{2,66},{4,68},{6,70},{8,72},{10,74},{12,76},{14,78},{16,80}... | collective-permute-start | bytes 129032 | tf_op jit(solution)/shard_map/ppermute | solution.py:52
  106.4 4.5 %collective-permute-start.23 = (bf16[1,24,896]{2,1,0:T(8,128)(2,1)S(1)}, bf16[1,24,896]{2,1,0:T(8,128)(2,1)S(1)}, u32[]{:S(2)}, u32[]{:S(2)}) collective-permute-start(bf16[1,24,896]{2,1,0:T(8,128)(2,1)S(1)} %add_convert_fusion.8), channel_id=1, source_target_pairs={{0,64},{2,66},{4,68},{6,70},{8,72},{10,74},{12,76},{14,78},{16,80}... | collective-permute-start | bytes 129032 | tf_op jit(solution)/shard_map/ppermute | solution.py:52
  110.9 7.2 %collective-permute-start.26 = (bf16[1,48,896]{2,1,0:T(8,128)(2,1)S(1)}, bf16[1,48,896]{2,1,0:T(8,128)(2,1)S(1)}, u32[]{:S(2)}, u32[]{:S(2)}) collective-permute-start(bf16[1,48,896]{2,1,0:T(8,128)(2,1)S(1)} %bitcast.155), channel_id=1, source_target_pairs={{0,8},{2,34},{4,12},{6,38},{8,0},{10,42},{12,4},{14,46},{16,24},{1... | collective-permute-start | bytes 258056 | tf_op jit(solution)/shard_map/ppermute | solution.py:52
  112.2 8.6 %collective-permute-start.25 = (bf16[1,48,896]{2,1,0:T(8,128)(2,1)S(1)}, bf16[1,48,896]{2,1,0:T(8,128)(2,1)S(1)}, u32[]{:S(2)}, u32[]{:S(2)}) collective-permute-start(bf16[1,48,896]{2,1,0:T(8,128)(2,1)S(1)} %bitcast.156), channel_id=1, source_target_pairs={{0,12},{2,50},{4,0},{6,54},{8,4},{10,58},{12,8},{14,62},{16,28},{1... | collective-permute-start | bytes 258056 | tf_op jit(solution)/shard_map/ppermute | solution.py:52
  112.8 8.0 %collective-permute-start.24 = (bf16[1,48,896]{2,1,0:T(8,128)(2,1)S(1)}, bf16[1,48,896]{2,1,0:T(8,128)(2,1)S(1)}, u32[]{:S(2)}, u32[]{:S(2)}) collective-permute-start(bf16[1,48,896]{2,1,0:T(8,128)(2,1)S(1)} %bitcast.157), channel_id=1, source_target_pairs={{0,4},{2,18},{4,8},{6,22},{8,12},{10,26},{12,0},{14,30},{16,20},{1... | collective-permute-start | bytes 258056 | tf_op jit(solution)/shard_map/ppermute | solution.py:52
  113.7 14.7 %collective-permute-start.12 = (bf16[512,768]{1,0:T(8,128)(2,1)S(1)}, bf16[512,768]{1,0:T(8,128)(2,1)}, u32[]{:S(2)}, u32[]{:S(2)}) collective-permute-start(bf16[512,768]{1,0:T(8,128)(2,1)S(1)} %get-tuple-element.212), channel_id=1, source_target_pairs={{0,1},{1,0},{2,3},{3,2},{4,5},{5,4},{6,7},{7,6},{8,9},{9,8},{10,11... | collective-permute-start | bytes 2359304 | tf_op jit(solution)/shard_map/ppermute | solution.py:656
  113.7 18.9 %collective-permute-start.31 = (bf16[2,192,768]{2,1,0:T(8,128)(2,1)S(1)}, bf16[2,192,768]{2,1,0:T(8,128)(2,1)S(1)}, u32[]{:S(2)}, u32[]{:S(2)}) collective-permute-start(bf16[2,192,768]{2,1,0:T(8,128)(2,1)S(1)} %bitcast.132), channel_id=1, source_target_pairs={{0,2},{2,0},{4,6},{6,4},{8,10},{10,8},{12,14},{14,12},{16,18},{18,... | collective-permute-start | bytes 1769480 | tf_op jit(solution)/shard_map/ppermute | solution.py:52
  118.1 15.8 %collective-permute-start.30 = (bf16[2,192,768]{2,1,0:T(8,128)(2,1)S(1)}, bf16[2,192,768]{2,1,0:T(8,128)(2,1)}, u32[]{:S(2)}, u32[]{:S(2)}) collective-permute-start(bf16[2,192,768]{2,1,0:T(8,128)(2,1)S(1)} %bitcast.133), channel_id=1, source_target_pairs={{0,48},{2,14},{4,52},{6,2},{8,56},{10,6},{12,60},{14,10},{16,0},{1... | collective-permute-start | bytes 1769480 | tf_op jit(solution)/shard_map/ppermute | solution.py:52
  120.8 13.2 %collective-permute-start.29 = (bf16[2,192,768]{2,1,0:T(8,128)(2,1)S(1)}, bf16[2,192,768]{2,1,0:T(8,128)(2,1)}, u32[]{:S(2)}, u32[]{:S(2)}) collective-permute-start(bf16[2,192,768]{2,1,0:T(8,128)(2,1)S(1)} %bitcast.134), channel_id=1, source_target_pairs={{0,32},{2,10},{4,36},{6,14},{8,40},{10,2},{12,44},{14,6},{16,48},{... | collective-permute-start | bytes 1769480 | tf_op jit(solution)/shard_map/ppermute | solution.py:52
  120.8 19.0 %collective-permute-start.28 = (bf16[2,192,768]{2,1,0:T(8,128)(2,1)S(1)}, bf16[2,192,768]{2,1,0:T(8,128)(2,1)}, u32[]{:S(2)}, u32[]{:S(2)}) collective-permute-start(bf16[2,192,768]{2,1,0:T(8,128)(2,1)S(1)} %bitcast.135), channel_id=1, source_target_pairs={{0,16},{2,6},{4,20},{6,10},{8,24},{10,14},{12,28},{14,2},{16,32},{... | collective-permute-start | bytes 1769480 | tf_op jit(solution)/shard_map/ppermute | solution.py:52
  128.4 12.0 %collective-permute-start.37 = (bf16[1,192,896]{2,1,0:T(8,128)(2,1)S(1)}, bf16[1,192,896]{2,1,0:T(8,128)(2,1)S(1)}, u32[]{:S(2)}, u32[]{:S(2)}) collective-permute-start(bf16[1,192,896]{2,1,0:T(8,128)(2,1)S(1)} %bitcast.138), channel_id=1, source_target_pairs={{0,48},{2,14},{4,52},{6,2},{8,56},{10,6},{12,60},{14,10},{16,0},{1... | collective-permute-start | bytes 1032200 | tf_op jit(solution)/shard_map/ppermute | solution.py:52
  132.6 28.9 %collective-permute-start.27 = (bf16[512,768]{1,0:T(8,128)(2,1)S(1)}, bf16[512,768]{1,0:T(8,128)(2,1)}, u32[]{:S(2)}, u32[]{:S(2)}) collective-permute-start(bf16[512,768]{1,0:T(8,128)(2,1)S(1)} %get-tuple-element.224), channel_id=1, source_target_pairs={{0,1},{1,0},{2,3},{3,2},{4,5},{5,4},{6,7},{7,6},{8,9},{9,8},{10,11... | collective-permute-start | bytes 2359304 | tf_op jit(solution)/shard_map/ppermute | solution.py:673
  133.9 7.9 %collective-permute-start.36 = (bf16[1,192,896]{2,1,0:T(8,128)(2,1)S(1)}, bf16[1,192,896]{2,1,0:T(8,128)(2,1)S(1)}, u32[]{:S(2)}, u32[]{:S(2)}) collective-permute-start(bf16[1,192,896]{2,1,0:T(8,128)(2,1)S(1)} %bitcast.139), channel_id=1, source_target_pairs={{0,32},{2,10},{4,36},{6,14},{8,40},{10,2},{12,44},{14,6},{16,48},{... | collective-permute-start | bytes 1032200 | tf_op jit(solution)/shard_map/ppermute | solution.py:52
  133.9 20.6 %collective-permute-start.34 = (bf16[2,192,768]{2,1,0:T(8,128)(2,1)}, bf16[2,192,768]{2,1,0:T(8,128)(2,1)}, u32[]{:S(2)}, u32[]{:S(2)}) collective-permute-start(bf16[2,192,768]{2,1,0:T(8,128)(2,1)} %collective-permute-done.30.refs_3_), channel_id=1, source_target_pairs={{0,2},{2,0},{4,6},{6,4},{8,10},{10,8},{12,14},{14,12},{16,18},{18,... | collective-permute-start | bytes 1769480 | tf_op jit(solution)/shard_map/ppermute | solution.py:52
  139.8 14.8 %collective-permute-start.33 = (bf16[2,192,768]{2,1,0:T(8,128)(2,1)}, bf16[2,192,768]{2,1,0:T(8,128)(2,1)}, u32[]{:S(2)}, u32[]{:S(2)}) collective-permute-start(bf16[2,192,768]{2,1,0:T(8,128)(2,1)} %collective-permute-done.29.refs_2_), channel_id=1, source_target_pairs={{0,2},{2,0},{4,6},{6,4},{8,10},{10,8},{12,14},{14,12},{16,18},{18,... | collective-permute-start | bytes 1769480 | tf_op jit(solution)/shard_map/ppermute | solution.py:52
  140.3 14.7 %collective-permute-start.32 = (bf16[2,192,768]{2,1,0:T(8,128)(2,1)}, bf16[2,192,768]{2,1,0:T(8,128)(2,1)}, u32[]{:S(2)}, u32[]{:S(2)}) collective-permute-start(bf16[2,192,768]{2,1,0:T(8,128)(2,1)} %collective-permute-done.28.refs_1_), channel_id=1, source_target_pairs={{0,2},{2,0},{4,6},{6,4},{8,10},{10,8},{12,14},{14,12},{16,18},{18,... | collective-permute-start | bytes 1769480 | tf_op jit(solution)/shard_map/ppermute | solution.py:52
  141.8 0.7 copy-start
  142.6 11.1 %collective-permute-start.35 = (bf16[1,192,896]{2,1,0:T(8,128)(2,1)S(1)}, bf16[1,192,896]{2,1,0:T(8,128)(2,1)}, u32[]{:S(2)}, u32[]{:S(2)}) collective-permute-start(bf16[1,192,896]{2,1,0:T(8,128)(2,1)S(1)} %bitcast.140), channel_id=1, source_target_pairs={{0,16},{2,6},{4,20},{6,10},{8,24},{10,14},{12,28},{14,2},{16,32},{... | collective-permute-start | bytes 1032200 | tf_op jit(solution)/shard_map/ppermute | solution.py:52
  145.3 9.3 %copy-start.1 = (bf16[1,192,896]{2,1,0:T(8,128)(2,1)S(1)}, bf16[1,192,896]{2,1,0:T(8,128)(2,1)}, u32[]{:S(2)}) copy-start(bf16[1,192,896]{2,1,0:T(8,128)(2,1)} %copy-done) | copy-start | bytes 1032196
  148.0 13.5 %copy-start.17 = (f32[512,768]{1,0:T(8,128)S(1)}, f32[512,768]{1,0:T(8,128)}, u32[]{:S(2)}) copy-start(f32[512,768]{1,0:T(8,128)} %cot_ref) | copy-start | bytes 4718596
  153.7 10.4 %collective-permute-start.38 = (bf16[1,192,896]{2,1,0:T(8,128)(2,1)S(1)}, bf16[1,192,896]{2,1,0:T(8,128)(2,1)S(1)}, u32[]{:S(2)}, u32[]{:S(2)}) collective-permute-start(bf16[1,192,896]{2,1,0:T(8,128)(2,1)S(1)} %bitcast.141), channel_id=1, source_target_pairs={{0,2},{2,0},{4,6},{6,4},{8,10},{10,8},{12,14},{14,12},{16,18},{18,... | collective-permute-start | bytes 1032200 | tf_op jit(solution)/shard_map/ppermute | solution.py:52
  154.5 9.5 %collective-permute-start.41 = (bf16[1,192,896]{2,1,0:T(8,128)(2,1)S(1)}, bf16[1,192,896]{2,1,0:T(8,128)(2,1)S(1)}, u32[]{:S(2)}, u32[]{:S(2)}) collective-permute-start(bf16[1,192,896]{2,1,0:T(8,128)(2,1)S(1)} %collective-permute-done.37.refs_3_), channel_id=1, source_target_pairs={{0,2},{2,0},{4,6},{6,4},{8,10},{10,8},{12,14},{14,12},{16,18},{18,... | collective-permute-start | bytes 1032200 | tf_op jit(solution)/shard_map/ppermute | solution.py:52
  154.6 9.5 %collective-permute-start.40 = (bf16[1,192,896]{2,1,0:T(8,128)(2,1)S(1)}, bf16[1,192,896]{2,1,0:T(8,128)(2,1)S(1)}, u32[]{:S(2)}, u32[]{:S(2)}) collective-permute-start(bf16[1,192,896]{2,1,0:T(8,128)(2,1)S(1)} %copy-done.1), channel_id=1, source_target_pairs={{0,2},{2,0},{4,6},{6,4},{8,10},{10,8},{12,14},{14,12},{16,18},{18,... | collective-permute-start | bytes 1032200 | tf_op jit(solution)/shard_map/ppermute | solution.py:52
  155.1 9.0 %collective-permute-start.39 = (bf16[1,192,896]{2,1,0:T(8,128)(2,1)}, bf16[1,192,896]{2,1,0:T(8,128)(2,1)S(1)}, u32[]{:S(2)}, u32[]{:S(2)}) collective-permute-start(bf16[1,192,896]{2,1,0:T(8,128)(2,1)} %collective-permute-done.35.refs_1_), channel_id=1, source_target_pairs={{0,2},{2,0},{4,6},{6,4},{8,10},{10,8},{12,14},{14,12},{16,18},{18,... | collective-permute-start | bytes 1032200 | tf_op jit(solution)/shard_map/ppermute | solution.py:52
  169.2 1.4 copy-start.18
